TPU v7x, 256 devices: a whole 4x4x8 slice. The times are simulated.
256 devices in a mesh: gy: 8 (over y_hi, x), gx: 32 (over y_lo, z, core).
Axes of the slice: x: 4, y: 4 (y_hi: 2, y_lo: 2; y = y_hi * 2 + y_lo), z: 8, core: 2. Of those that a mesh axis runs over, the one named last changes fastest.
Arguments:
- queries: bfloat16 [128, 512, 512], P('gy', 'gx'), may hold values from -7 to 7
- key_vectors: bfloat16 [128, 512, 512], P('gy', 'gx'), may hold values from -7 to 7
- values: bfloat16 [128, 512, 512], P('gy', 'gx'), may hold values from -6 to 6
- residual: bfloat16 [128, 512, 512], P('gy', 'gx'), may hold values from -60 to 60
- cotangent: bfloat16 [128, 512, 512], P('gy', 'gx'), may hold values from -6 to 6
- out_proj: bfloat16 [512, 512], replicated, may hold values from -0.25 to 0.25
- norm_gain: float32 [512], replicated, may hold values from 0.5 to 1.5
- router: bfloat16 [512, 64], replicated, may hold values from -0.25 to 0.25
- expert_in: bfloat16 [64, 512, 2048], P('gx'), may hold values from -0.25 to 0.25
- expert_out: bfloat16 [64, 2048, 512], P('gx'), may hold values from -0.125 to 0.125
- expert_id: int32 [128, 512], P('gy', 'gx'), may hold values from 0 to 63, as said below
- slot_index: int32 [128, 512], P('gy', 'gx'), may hold values from 0 to 7
Outputs:
- grad_queries: bfloat16 [128, 512, 512], P('gy', 'gx')
- grad_keys: bfloat16 [128, 512, 512], P('gy', 'gx')
- grad_values: bfloat16 [128, 512, 512], P('gy', 'gx')
- grad_input: bfloat16 [128, 512, 512], P('gy', 'gx')
- grad_out_proj: bfloat16 [512, 512], replicated
- grad_gain: float32 [512], replicated
- grad_router: float32 [512, 64], replicated
- grad_expert_in: bfloat16 [64, 512, 2048], P('gx', None, 'gy')
- grad_expert_out: bfloat16 [64, 2048, 512], P('gx', 'gy')
Inputs may be any that keep to these rules, and one draw needn't show every extreme that they name: `expert_id`: within each aligned 16 x 16 tile no two tokens share both expert and slot, so an expert has at most 8 tokens of a tile; in every row of tiles one expert fills all 8 of its slots in every tile of that row.
All inputs are finite; a program needn't handle non-finite values.
Results may differ from a plain program's by a relative error of at most 0.015.
Values may be sent and summed in bfloat16 or wider, within the bound.
No kernel may reach another device: no remote copies, remote signals or barrier semaphores. Data moves between devices by JAX's collectives and lax.ppermute only.
A program may use at most 128 MiB of HBM per device.

v0:
```python
import functools

import jax
import jax.numpy as jnp
from jax import lax
from jax.experimental import pallas as pl
from jax.experimental.pallas import tpu as pltpu
from jax.sharding import Mesh
from jax.sharding import PartitionSpec as P

HEADS = 16
EPSILON = 1e-05
NEGATIVE = -1e30
GELU_COEF = 0.7978845608028654
CUBIC_COEF = 0.044715
GY = ("yh", "x")
GX = ("g", "c")
EVERY = GY + GX
ANY = pl.BlockSpec(memory_space=pl.ANY)
VMEM = pl.BlockSpec(memory_space=pltpu.VMEM)
SMEM = pl.BlockSpec(memory_space=pltpu.SMEM)


def fetch(block, down, right):
    rows, cols = lax.axis_size(GY), lax.axis_size(GX)
    if down == 0 and right == 0:
        return block
    if down == 0:
        return lax.ppermute(block, GX, [((j + right) % cols, j) for j in range(cols)])
    if right == 0:
        return lax.ppermute(block, GY, [((i + down) % rows, i) for i in range(rows)])
    route = [
        (((i + down) % rows) * cols + (j + right) % cols, i * cols + j)
        for i in range(rows)
        for j in range(cols)
    ]
    return lax.ppermute(block, EVERY, route)


def swap(block, axis):
    return lax.ppermute(block, axis, [(0, 1), (1, 0)])


def step(block, way):
    size = lax.axis_size("x")
    return lax.ppermute(block, "x", [(i, (i + way) % size) for i in range(size)])


def image_to_window(quarters):
    return [fetch(quarters[3 - p], p // 2, p % 2) for p in range(4)]


def window_to_image(pieces):
    return [fetch(pieces[3 - q], -((3 - q) // 2), -((3 - q) % 2)) for q in range(4)]


def gelu_parts(inputs):
    square = inputs * inputs
    factor = GELU_COEF + (GELU_COEF * CUBIC_COEF) * square
    tangent = jnp.tanh(inputs * factor)
    share = 0.5 + 0.5 * tangent
    value = inputs * share
    slope = share + value * (1.0 - tangent) * (3.0 * factor - 2.0 * GELU_COEF)
    return value, slope

NN = (((1,), (0,)), ((), ()))
NT = (((1,), (1,)), ((), ()))
TN = (((0,), (0,)), ((), ()))
GROUP = 128


def mul(a, b, dims):
    return lax.dot_general(a, b, dims, preferred_element_type=jnp.float32)


def window_parts(pieces, quarter):
    return [
        jnp.concatenate([p[quarter * n : quarter * (n + 1), :] for p in pieces], axis=0) for n in range(3)
    ]


def attend_kernel(quarter, head_size, last_ref, *refs):
    pieces, mixed_refs, probs_ref = refs[:4], refs[-5:-1], refs[-1]
    query, key, value = window_parts(pieces, quarter)
    tokens = query.shape[0]
    of_key = lax.broadcasted_iota(jnp.int32, (tokens, tokens), 0)
    of_query = lax.broadcasted_iota(jnp.int32, (tokens, tokens), 1)
    differs = jnp.bitwise_xor(of_key // quarter, of_query // quarter)
    hidden = jnp.bitwise_and(differs, last_ref[0]) != 0
    scale = head_size ** (-0.5)
    lane_head = lax.broadcasted_iota(jnp.int32, query.shape, 1) // head_size
    value_t = value.T
    mixed_t = []
    for h in range(GROUP // head_size):
        masked = jnp.where(lane_head == h, query, jnp.zeros_like(query))
        scores = mul(key, masked, NT) * scale
        scores = jnp.where(hidden, NEGATIVE, scores)
        weights = jnp.exp(scores - jnp.max(scores, axis=0, keepdims=True))
        probs = (weights * (1.0 / jnp.sum(weights, axis=0, keepdims=True))).astype(jnp.bfloat16)
        probs_ref[h] = probs
        mixed_t.append(mul(value_t[h * head_size : (h + 1) * head_size, :], probs, NN))
    mixed = jnp.concatenate(mixed_t, axis=0).T.astype(jnp.bfloat16)
    for p in range(4):
        mixed_refs[p][...] = mixed[quarter * p : quarter * (p + 1), :]


def attend_back_kernel(quarter, head_size, *refs):
    pieces, grad_refs, probs_ref, outs = refs[:4], refs[4:8], refs[8], refs[-4:]
    query, key, value = window_parts(pieces, quarter)
    grad = jnp.concatenate([r[...] for r in grad_refs], axis=0)
    scale = head_size ** (-0.5)
    lane_head = lax.broadcasted_iota(jnp.int32, query.shape, 1) // head_size
    key_t = key.T
    grad_query_t = []
    grad_key = jnp.zeros(query.shape, jnp.float32)
    grad_value = jnp.zeros(query.shape, jnp.float32)
    for h in range(GROUP // head_size):
        mine = lane_head == h
        masked_grad = jnp.where(mine, grad, jnp.zeros_like(grad))
        masked_query = jnp.where(mine, query, jnp.zeros_like(query))
        probs_low = probs_ref[h]
        probs = probs_low.astype(jnp.float32)
        grad_probs = mul(value, masked_grad, NT)
        total = jnp.sum(probs * grad_probs, axis=0, keepdims=True)
        grad_scores = (probs * (grad_probs - total) * scale).astype(jnp.bfloat16)
        grad_value += mul(probs_low, masked_grad, NN)
        grad_key += mul(grad_scores, masked_query, NN)
        grad_query_t.append(mul(key_t[h * head_size : (h + 1) * head_size, :], grad_scores, NN))
    grad_query = jnp.concatenate(grad_query_t, axis=0).T
    for n, g in enumerate((grad_query, grad_key, grad_value)):
        low = g.astype(jnp.bfloat16)
        for p in range(4):
            outs[p][quarter * n : quarter * (n + 1), :] = low[quarter * p : quarter * (p + 1), :]


def staged(kernel, count, *refs):
    inputs, (buffers, sems) = refs[:count], (refs[-1 - count : -1], refs[-1])
    copies = [pltpu.make_async_copy(inputs[n], buffers[n], sems.at[n]) for n in range(count)]
    for copy in copies:
        copy.start()
    for copy in copies:
        copy.wait()
    kernel(*buffers, *refs[count : -1 - count])


def on_staged(kernel, inputs, earlier, out_shape, name, flops=0):
    return pl.pallas_call(
        functools.partial(staged, kernel, len(inputs)),
        in_specs=[ANY] * (len(inputs) + len(earlier)),
        out_shape=out_shape,
        scratch_shapes=[pltpu.VMEM(x.shape, x.dtype) for x in inputs]
        + [pltpu.SemaphoreType.DMA((len(inputs),))],
        compiler_params=params(),
        cost_estimate=pl.CostEstimate(flops=flops, bytes_accessed=1, transcendentals=0),
        name=name,
    )(*inputs, *earlier)


def params():
    return pltpu.CompilerParams(vmem_limit_bytes=60 * 1024 * 1024)


def attend(last, pieces, quarter, head_size):
    tokens, width = 4 * quarter, pieces[0].shape[1]
    heads, groups = GROUP // head_size, width // GROUP
    return pl.pallas_call(
        functools.partial(attend_kernel, quarter, head_size),
        grid=(groups,),
        in_specs=[SMEM]
        + [pl.BlockSpec((3 * quarter, GROUP), lambda g: (0, g))] * 4,
        out_specs=[pl.BlockSpec((quarter, GROUP), lambda g: (0, g))] * 4
        + [pl.BlockSpec((heads, tokens, tokens), lambda g: (g, 0, 0))],
        out_shape=[jax.ShapeDtypeStruct((quarter, width), jnp.bfloat16)] * 4
        + [jax.ShapeDtypeStruct((width // head_size, tokens, tokens), jnp.bfloat16)],
        compiler_params=params(),
        cost_estimate=pl.CostEstimate(
            flops=16 * tokens * tokens * width, bytes_accessed=12 * tokens * width, transcendentals=0
        ),
        name="attend",
    )(last, *pieces)


def attend_back(pieces, grads, probs, quarter, head_size, earlier):
    tokens, width = 4 * quarter, pieces[0].shape[1]
    heads, groups = GROUP // head_size, width // GROUP
    return pl.pallas_call(
        functools.partial(attend_back_kernel, quarter, head_size),
        grid=(groups,),
        in_specs=[pl.BlockSpec((3 * quarter, GROUP), lambda g: (0, g))] * 4
        + [pl.BlockSpec((quarter, GROUP), lambda g: (0, g))] * 4
        + [pl.BlockSpec((heads, tokens, tokens), lambda g: (g, 0, 0))]
        + [ANY] * len(earlier),
        out_specs=[pl.BlockSpec((3 * quarter, GROUP), lambda g: (0, g))] * 4,
        out_shape=[jax.ShapeDtypeStruct((3 * quarter, width), jnp.bfloat16)] * 4,
        compiler_params=params(),
        cost_estimate=pl.CostEstimate(
            flops=8 * tokens * tokens * width * 4, bytes_accessed=12 * tokens * width * 2, transcendentals=0
        ),
        name="attend_back",
    )(*pieces, *grads, probs, *earlier)


def bring(sources, buffers, sems):
    copies = [pltpu.make_async_copy(s, b, sems.at[n]) for n, (s, b) in enumerate(zip(sources, buffers))]
    for copy in copies:
        copy.start()
    return copies


def expert_kernel(chunk, hidden_hbm, cot_hbm, router_hbm, gain_hbm, in_hbm, out_hbm, *refs):
    back_ref, small_ref, ins, outs, sems, hidden_ref, cot_ref, router_ref, gain_ref, few_sems = refs[-10:]
    f32 = jnp.float32
    count, chunks = ins.shape[:2]
    few = bring(
        (hidden_hbm, router_hbm, cot_hbm, gain_hbm), (hidden_ref, router_ref, cot_ref, gain_ref), few_sems
    )
    copies = {}
    for e in range(count):
        for c in range(chunks):
            units = pl.ds(chunk * c, chunk)
            copies[e, c] = (
                pltpu.make_async_copy(in_hbm.at[e, :, units], ins.at[e, c], sems.at[0, e, c]),
                pltpu.make_async_copy(out_hbm.at[e, units, :], outs.at[e, c], sems.at[1, e, c]),
            )
            for copy in copies[e, c]:
                copy.start()
    for copy in few:
        copy.wait()
    for e in range(count):
        slots = hidden_ref[e]
        wide = slots.astype(f32)
        router_row = router_ref[e]
        logit = jnp.sum(wide * router_row, axis=-1, keepdims=True)
        gate = 1.0 / (1.0 + jnp.exp(-logit))
        gate_low = gate.astype(jnp.bfloat16).astype(f32)
        total, gate_sum = 0.0, 0.0
        for c in range(chunks):
            for copy in copies[e, c]:
                copy.wait()
            weight, spread = ins[e, c], mul(cot_ref[e], outs[e, c], NT)
            activated, slope = gelu_parts(mul(slots, weight, NN))
            gate_sum += jnp.sum(activated * spread, axis=-1, keepdims=True)
            total += mul((gate_low * spread * slope).astype(jnp.bfloat16), weight, NT)
        grad_logit = gate_sum * gate * (1.0 - gate)
        grad_hidden = total + grad_logit * router_row
        back_ref[e] = grad_hidden.astype(jnp.bfloat16)
        small_ref[e, 0:1, :] = jnp.sum(wide * grad_logit, axis=0, keepdims=True)
        small_ref[e, 1:2, :] = jnp.sum(wide * grad_hidden, axis=0, keepdims=True) / gain_ref[...]


def experts(slot_hidden, slot_cot, expert_in, expert_out, router_rows, gain, earlier):
    count, slots, width = slot_hidden.shape
    hidden = expert_in.shape[2]
    chunk = min(hidden, 512)
    chunks = hidden // chunk
    return pl.pallas_call(
        functools.partial(expert_kernel, chunk),
        in_specs=[ANY] * (6 + len(earlier)),
        out_shape=[
            jax.ShapeDtypeStruct((count, slots, width), jnp.bfloat16),
            jax.ShapeDtypeStruct((count, 2, width), jnp.float32),
        ],
        scratch_shapes=[
            pltpu.VMEM((count, chunks, width, chunk), jnp.bfloat16),
            pltpu.VMEM((count, chunks, chunk, width), jnp.bfloat16),
            pltpu.SemaphoreType.DMA((2, count, chunks)),
            pltpu.VMEM(slot_hidden.shape, slot_hidden.dtype),
            pltpu.VMEM(slot_cot.shape, slot_cot.dtype),
            pltpu.VMEM(router_rows.shape, router_rows.dtype),
            pltpu.VMEM(gain.shape, gain.dtype),
            pltpu.SemaphoreType.DMA((4,)),
        ],
        compiler_params=params(),
        cost_estimate=pl.CostEstimate(
            flops=12 * count * slots * width * hidden, bytes_accessed=8 * count * slots * hidden, transcendentals=0
        ),
        name="experts",
    )(slot_hidden, slot_cot, router_rows, gain, expert_in, expert_out, *earlier)


def weights_kernel(units_ref, *refs):
    f32, bf16 = jnp.float32, jnp.bfloat16
    in_hbm, out_hbm = refs[5:7]
    far_in_ref, far_out_ref, up_ref, down_ref, own_ref, token_ref, ins, outs, sems = refs[-15:-6]
    hidden_refs, cot_refs, router_ref = refs[-6:-4], refs[-4:-2], refs[-2]
    few = bring(refs[:5], refs[-6:-1], refs[-1])
    count, ways, width, part = ins.shape
    copies = {}
    for e in range(count):
        for d in range(ways):
            units = pl.ds(pl.multiple_of(units_ref[d] * part, part), part)
            copies[e, d] = (
                pltpu.make_async_copy(in_hbm.at[e, :, units], ins.at[e, d], sems.at[0, e, d]),
                pltpu.make_async_copy(out_hbm.at[e, units, :], outs.at[e, d], sems.at[1, e, d]),
            )
            for copy in copies[e, d]:
                copy.start()
    token_ref[...] = jnp.zeros_like(token_ref)
    for copy in few:
        copy.wait()
    for e in range(count):
        slots = jnp.concatenate([r[e] for r in hidden_refs], axis=0)
        cot = jnp.concatenate([r[e] for r in cot_refs], axis=0)
        logit = jnp.sum(slots.astype(f32) * router_ref[e], axis=-1, keepdims=True)
        gate = (1.0 / (1.0 + jnp.exp(-logit))).astype(bf16).astype(f32)
        scaled = (gate * cot.astype(f32)).astype(bf16)
        slots_t, scaled_t = slots.T, scaled.T
        for d in range(ways):
            for copy in copies[e, d]:
                copy.wait()
            activated, slope = gelu_parts(mul(slots, ins[e, d], NN))
            grad_pre = (mul(scaled, outs[e, d], NT) * slope).astype(bf16)
            sum_in = mul(slots_t, grad_pre, NN)
            sum_out = mul(scaled_t, activated.astype(bf16), NN)
            if d == 0:
                far_in_ref[e] = sum_in.astype(bf16)
                far_out_ref[e] = sum_out.astype(bf16)
            else:
                target = (up_ref, down_ref, own_ref)[d - 1]
                target[0, e] = sum_in.astype(target.dtype)
                target[1, e] = sum_out.astype(target.dtype)


def weight_sums(hidden_rows, cot_rows, router_rows, expert_in, expert_out, earlier):
    count, slots, width = hidden_rows[0].shape
    along = lax.axis_size("x")
    part = expert_in.shape[2] // (2 * along)
    half, place = lax.axis_index("yh"), lax.axis_index("x")
    units = jnp.stack([half * along + (place + way) % along for way in (2, 1, -1, 0)]).astype(jnp.int32)
    bf16, f32 = jnp.bfloat16, jnp.float32
    return pl.pallas_call(
        weights_kernel,
        in_specs=[SMEM] + [ANY] * (7 + len(earlier)),
        out_shape=[jax.ShapeDtypeStruct((count, width, part), bf16)] * 2
        + [jax.ShapeDtypeStruct((2, count, width, part), t) for t in (bf16, bf16, f32)]
        + [jax.ShapeDtypeStruct((8, 128), f32)],
        scratch_shapes=[
            pltpu.VMEM((count, 4, width, part), bf16),
            pltpu.VMEM((count, 4, part, width), bf16),
            pltpu.SemaphoreType.DMA((2, count, 4)),
        ]
        + [pltpu.VMEM((count, slots, width), bf16)] * 4
        + [pltpu.VMEM(router_rows.shape, f32), pltpu.SemaphoreType.DMA((5,))],
        compiler_params=params(),
        cost_estimate=pl.CostEstimate(
            flops=128 * count * slots * width * part, bytes_accessed=16 * count * slots * width, transcendentals=0
        ),
        name="weight_sums",
    )(units, *hidden_rows, *cot_rows, router_rows, expert_in, expert_out, *earlier)


def join_kernel(up_ref, down_ref, far_in_ref, far_out_ref, *refs):
    up_out, down_out = refs[-2:]
    f32, bf16 = jnp.float32, jnp.bfloat16
    up_out[0] = (up_ref[0].astype(f32) + far_in_ref[...].astype(f32)).astype(bf16)
    up_out[1] = up_ref[1]
    down_out[0] = down_ref[0]
    down_out[1] = (down_ref[1].astype(f32) + far_out_ref[...].astype(f32)).astype(bf16)


def join(up, down, far_in, far_out, earlier):
    return on_staged(
        join_kernel,
        (up, down, far_in, far_out),
        earlier,
        [jax.ShapeDtypeStruct(up.shape, up.dtype)] * 2,
        "join",
    )


def weight_total_kernel(own_ref, up_ref, down_ref, grad_in_ref, grad_out_ref):
    f32 = jnp.float32
    total = own_ref[:, 0] + up_ref[:, 0].astype(f32) + down_ref[:, 0].astype(f32)
    grad_in_ref[0] = total[0].astype(jnp.bfloat16)
    grad_out_ref[0] = total[1].T.astype(jnp.bfloat16)


def weight_total(own, up, down):
    _, count, width, part = own.shape
    arrived = pl.BlockSpec((2, 1, width, part), lambda e: (0, e, 0, 0))
    return pl.pallas_call(
        weight_total_kernel,
        grid=(count,),
        in_specs=[arrived] * 3,
        out_specs=[
            pl.BlockSpec((1, width, part), lambda e: (e, 0, 0)),
            pl.BlockSpec((1, part, width), lambda e: (e, 0, 0)),
        ],
        out_shape=[
            jax.ShapeDtypeStruct((count, width, part), jnp.bfloat16),
            jax.ShapeDtypeStruct((count, part, width), jnp.bfloat16),
        ],
        compiler_params=params(),
        name="weight_total",
    )(own, up, down)


def quarter_of(tile_ref, q):
    half = tile_ref.shape[0] // 2
    a, b = q // 2, q % 2
    block = tile_ref[half * a : half * (a + 1), half * b : half * (b + 1), :]
    return block.reshape(half * half, tile_ref.shape[2])


def quarters_kernel(count, *refs):
    outs, (buffer, sems) = refs[count : count + 4], refs[-2:]
    copies = [pltpu.make_async_copy(refs[n], buffer.at[n], sems.at[n]) for n in range(count)]
    for copy in copies:
        copy.start()
    for n in range(count):
        copies[n].wait()
        for q in range(4):
            block = quarter_of(buffer.at[n], q)
            rows = block.shape[0]
            outs[q][rows * n : rows * (n + 1), :] = block


def quarters(tiles):
    side, _, width = tiles[0].shape
    count = len(tiles)
    return pl.pallas_call(
        functools.partial(quarters_kernel, count),
        in_specs=[ANY] * count,
        out_shape=[jax.ShapeDtypeStruct((count * side * side // 4, width), tiles[0].dtype)] * 4,
        scratch_shapes=[
            pltpu.VMEM((count, side, side, width), tiles[0].dtype),
            pltpu.SemaphoreType.DMA((count,)),
        ],
        compiler_params=params(),
        name="quarters",
    )(*tiles)


def tiles_kernel(count, *refs):
    for n in range(count):
        tile_ref = refs[4 + n]
        half, width = tile_ref.shape[0] // 2, tile_ref.shape[2]
        for q in range(4):
            a, b = q // 2, q % 2
            block = refs[q][half * half * n : half * half * (n + 1), :].reshape(half, half, width)
            tile_ref[half * a : half * (a + 1), half * b : half * (b + 1), :] = block


def tiles(parts, count, side):
    width = parts[0].shape[1]
    return pl.pallas_call(
        functools.partial(tiles_kernel, count),
        grid=(width // GROUP,),
        in_specs=[pl.BlockSpec((parts[0].shape[0], GROUP), lambda g: (0, g))] * 4,
        out_specs=[pl.BlockSpec((side, side, GROUP), lambda g: (0, 0, g))] * count,
        out_shape=[jax.ShapeDtypeStruct((side, side, width), parts[0].dtype)] * count,
        compiler_params=params(),
        name="tiles",
    )(*parts)


def slot_picker(place_ref, slots):
    place = place_ref[...]
    index = lax.broadcasted_iota(jnp.int32, (slots, place.shape[1]), 0)
    return (index == place).astype(jnp.bfloat16)


def to_slots_kernel(place_ref, cot_hbm, residual_hbm, *refs):
    slots_ref, cot_ref, residual_ref, buffer, sems = refs[-5:]
    copies = [
        pltpu.make_async_copy(hbm, buffer.at[n], sems.at[n]) for n, hbm in enumerate((cot_hbm, residual_hbm))
    ]
    for copy in copies:
        copy.start()
    for n, out in enumerate((cot_ref, residual_ref)):
        copies[n].wait()
        for q in range(4):
            block = quarter_of(buffer.at[n], q)
            rows = block.shape[0]
            out[rows * q : rows * (q + 1), :] = block
        if n == 0:
            picker = slot_picker(place_ref, slots_ref.shape[0])
            slots_ref[...] = mul(picker, cot_ref[...], NN).astype(slots_ref.dtype)


def to_slots(place, cotangent, residual, slots, earlier):
    side, _, width = cotangent.shape
    low = cotangent.dtype
    return pl.pallas_call(
        to_slots_kernel,
        in_specs=[VMEM, ANY, ANY] + [ANY] * len(earlier),
        out_shape=[jax.ShapeDtypeStruct((slots, width), low)]
        + [jax.ShapeDtypeStruct((side * side, width), low)] * 2,
        scratch_shapes=[pltpu.VMEM((2, side, side, width), low), pltpu.SemaphoreType.DMA((2,))],
        compiler_params=params(),
        name="to_slots",
    )(place, cotangent, residual, *earlier)


def norm_kernel(place_ref, gain_ref, proj_ref, *refs):
    f32, bf16 = jnp.float32, jnp.bfloat16
    mixed_refs = refs[:4]
    residual_ref, slots_ref, normed_ref, inv_ref = refs[4], *refs[-3:]
    mixed = jnp.concatenate([r[...] for r in mixed_refs], axis=0)
    attended = mul(mixed, proj_ref[...], NN).astype(bf16)
    stream = residual_ref[...].astype(f32) + attended.astype(f32)
    centered = stream - jnp.mean(stream, axis=-1, keepdims=True)
    inv_std = lax.rsqrt(jnp.mean(centered * centered, axis=-1, keepdims=True) + EPSILON)
    normed = centered * inv_std
    hidden_in = (normed * gain_ref[...]).astype(bf16)
    normed_ref[...] = normed
    inv_ref[...] = inv_std
    slots_ref[...] = mul(slot_picker(place_ref, slots_ref.shape[0]), hidden_in, NN).astype(bf16)


def norm(place, gain, out_proj, mixed, residual, slots, earlier):
    tokens, width = place.shape[1], out_proj.shape[0]
    return on_staged(
        norm_kernel,
        (place, gain, out_proj, *mixed, residual),
        earlier,
        [
            jax.ShapeDtypeStruct((slots, width), jnp.bfloat16),
            jax.ShapeDtypeStruct((tokens, width), jnp.float32),
            jax.ShapeDtypeStruct((tokens, 1), jnp.float32),
        ],
        "norm",
    )


def token_kernel(place_ref, gain_ref, proj_ref, returned_ref, normed_ref, inv_ref, *refs):
    f32, bf16 = jnp.float32, jnp.bfloat16
    mixed_refs, cot_ref = refs[:4], refs[4]
    grad_refs, grad_mixed_refs, part_ref = refs[-9:-5], refs[-5:-1], refs[-1]
    mixed = jnp.concatenate([r[...] for r in mixed_refs], axis=0)
    cot = cot_ref[...]
    normed, inv_std = normed_ref[...], inv_ref[...]
    grad_hidden = mul(slot_picker(place_ref, returned_ref.shape[0]), returned_ref[...], TN)
    grad = grad_hidden * gain_ref[...]
    grad_input = (
        cot.astype(f32)
        + inv_std
        * (
            grad
            - jnp.mean(grad, axis=-1, keepdims=True)
            - normed * jnp.mean(grad * normed, axis=-1, keepdims=True)
        )
    ).astype(bf16)
    grad_mixed = mul(grad_input, proj_ref[...], NT).astype(bf16)
    part_ref[...] = mul(mixed, grad_input, TN).astype(bf16)
    quarter = grad_refs[0].shape[0]
    for q in range(4):
        grad_refs[q][...] = grad_input[quarter * q : quarter * (q + 1), :]
        grad_mixed_refs[q][...] = grad_mixed[quarter * q : quarter * (q + 1), :]


def token_grads(place, gain, out_proj, returned, normed, inv_std, mixed, cot, earlier):
    tokens, width = normed.shape
    return on_staged(
        token_kernel,
        (place, gain, out_proj, returned, normed, inv_std, *mixed, cot),
        earlier,
        [jax.ShapeDtypeStruct((tokens // 4, width), jnp.bfloat16)] * 8
        + [jax.ShapeDtypeStruct((width, width), jnp.bfloat16)],
        "token_grads",
    )


def to_devices_kernel(rows_ref, *refs):
    out_ref = refs[-1]
    devices, rows, width = out_ref.shape
    count = rows_ref.shape[0]
    parts = [
        rows_ref[e].astype(jnp.float32).reshape(devices, rows // count, width) for e in range(count)
    ]
    out_ref[...] = jnp.concatenate(parts, axis=1).astype(out_ref.dtype)


def to_devices(rows, devices, earlier):
    count, slots, width = rows.shape
    shape = jax.ShapeDtypeStruct((devices, count * slots // devices, width), rows.dtype)
    return on_staged(to_devices_kernel, (rows,), earlier, shape, "to_devices")


def finish_kernel(part, count, summed_ref, *refs):
    proj_ref, gain_ref, further_ref = refs[-3:]
    devices, _, width = summed_ref.shape
    proj_ref[...] = summed_ref[:, :part, :].reshape(devices * part, width)
    further = summed_ref[:, part:, :].astype(jnp.float32)
    further_ref[...] = further
    gain_ref[...] = jnp.sum(further[:, count, :], axis=0, keepdims=True)


def finish(summed, part, count, earlier):
    devices, rows, width = summed.shape
    return on_staged(
        functools.partial(finish_kernel, part, count),
        (summed,),
        earlier,
        [
            jax.ShapeDtypeStruct((devices * part, width), summed.dtype),
            jax.ShapeDtypeStruct((1, width), jnp.float32),
            jax.ShapeDtypeStruct((devices, rows - part, width), jnp.float32),
        ],
        "finish",
    )


def share_kernel(further, shares_ref, *refs):
    total = jnp.sum(shares_ref[...].astype(jnp.float32), axis=0)
    out_ref = refs[-1]
    total = jnp.concatenate([total] + [r[...] for r in refs[:further]], axis=0).astype(jnp.bfloat16)
    out_ref[...] = jnp.broadcast_to(total[None], out_ref.shape)


def share_sum(inputs, copies, earlier):
    rows = inputs[0].shape[1] + sum(x.shape[0] for x in inputs[1:])
    shape = jax.ShapeDtypeStruct((copies, rows, inputs[0].shape[2]), inputs[0].dtype)
    kernel = functools.partial(share_kernel, len(inputs) - 1)
    return on_staged(kernel, inputs, earlier, shape, "share_sum")


def shards(
    queries,
    key_vectors,
    values,
    residual,
    cotangent,
    out_proj,
    norm_gain,
    router,
    expert_in,
    expert_out,
    expert_id,
    slot_index,
):
    f32, bf16 = jnp.float32, jnp.bfloat16
    side = queries.shape[0]
    width = queries.shape[2]
    head_size = width // HEADS
    tokens = side * side
    quarter = tokens // 4
    expert_count = router.shape[1]
    local_experts = expert_in.shape[0]
    capacity = 2 * tokens // expert_count
    slots_total = expert_count * capacity
    grid_rows, grid_cols = lax.axis_size(GY), lax.axis_size(GX)
    row, col = lax.axis_index(GY), lax.axis_index(GX)
    core = lax.axis_index("c")
    gain = norm_gain[None, :]

    pieces = image_to_window(quarters([queries, key_vectors, values]))

    place = (
        (expert_id * capacity + slot_index)
        .reshape(2, side // 2, 2, side // 2)
        .transpose(0, 2, 1, 3)
        .reshape(1, tokens)
    )
    cot_slots, cot, residual = to_slots(place, cotangent, residual, slots_total, pieces[1:])

    def exchange(slots):
        arrived = lax.all_to_all(slots, GX, 0, 0, tiled=True)
        return (
            arrived.reshape(grid_cols, local_experts, capacity, width)
            .transpose(1, 0, 2, 3)
            .reshape(local_experts, grid_cols * capacity, width)
        )

    slot_cot = exchange(cot_slots)
    other_cot = swap(slot_cot, "yh")

    last = (2 * (row == grid_rows - 1) + (col == grid_cols - 1)).astype(jnp.int32)[None]
    *mixed_win, probs = attend(last, pieces, quarter, head_size)
    mixed = window_to_image(mixed_win)

    slots, normed, inv_std = norm(place, gain, out_proj, mixed, residual, slots_total, ())

    slot_hidden = exchange(slots)
    other_hidden = swap(slot_hidden, "yh")
    router_rows = lax.dynamic_slice_in_dim(router, col * local_experts, local_experts, 1).T.astype(f32)[:, None]
    grad_hidden_slot, small = experts(
        slot_hidden, slot_cot, expert_in, expert_out, router_rows, gain, (other_cot,)
    )
    returning = to_devices(grad_hidden_slot, grid_cols, (other_hidden,))
    returned = lax.all_to_all(returning, GX, 0, 0, tiled=True).reshape(slots_total, width)

    far_in, far_out, upward, downward, own_sums, sums_done = weight_sums(
        (slot_hidden, other_hidden),
        (slot_cot, other_cot),
        router_rows,
        expert_in,
        expert_out,
        (small,),
    )
    far_in, far_out = step(far_in, 1), step(far_out, -1)
    outcome = token_grads(place, gain, out_proj, returned, normed, inv_std, mixed, cot, (sums_done,))
    grad_input, grad_mixed_image, proj_part = outcome[:4], outcome[4:8], outcome[8]
    grad_mixed = image_to_window(grad_mixed_image)
    upward, downward = join(upward, downward, far_in, far_out, grad_mixed[1:])
    from_below, from_above = step(upward, 1), step(downward, -1)

    grads = attend_back(pieces, grad_mixed, probs, quarter, head_size, ())

    extra = jnp.concatenate((small[:, 0], jnp.sum(small[:, 1], axis=0, keepdims=True)), axis=0)
    extra = jnp.pad(extra, ((0, -extra.shape[0] % 8), (0, 0)))
    shares = lax.all_to_all(proj_part.reshape(grid_cols, -1, width), GX, 0, 0, tiled=True)
    shares = lax.all_to_all(share_sum((shares, extra), grid_rows, (grads[0], upward)), GY, 0, 0, tiled=True)
    summed = lax.all_to_all(share_sum((shares,), grid_cols, (from_below, from_above)), GX, 0, 0, tiled=True)
    image_out = tiles(window_to_image(grads), 3, side)
    grad_proj, grad_gain, further = finish(summed, width // grid_cols, local_experts, image_out[:1])
    grad_router = further[:, :local_experts].reshape(expert_count, width).T
    grad_in, grad_out = weight_total(own_sums, from_below, from_above)

    return (
        image_out[0],
        image_out[1],
        image_out[2],
        tiles(grad_input, 1, side)[0],
        grad_proj,
        grad_gain[0],
        grad_router,
        grad_in,
        grad_out,
    )


def solution(mesh):
    rows, cols = mesh.devices.shape
    split = Mesh(mesh.devices.reshape(2, rows // 2, cols // 2, 2), EVERY)
    tile = P(GY, GX, None)
    return jax.shard_map(
        shards,
        mesh=split,
        in_specs=(tile,) * 5 + (P(), P(), P(), P(GX, None, None), P(GX, None, None), P(GY, GX), P(GY, GX)),
        out_specs=(tile,) * 4 + (P(), P(), P(), P(GX, None, GY), P(GX, GY, None)),
        check_vma=False,
    )
```

profile of v0, /device:TPU:8, one launch (start us, length us, event | category | flops | bytes accessed | tf_op | source)
XLA Modules:
  0.0 229.8 jit_solution(3602806494361715217)
XLA Ops:
  0.6 2.0 quarters.1
  2.7 5.3 %collective-permute-start = (bf16[192,512]{1,0:T(8,128)(2,1)}, bf16[192,512]{1,0:T(8,128)(2,1)S(1)}, u32[]{:S(2)}, u32[]{:S(2)}) collective-permute-start(bf16[192,512]{1,0:T(8,128)(2,1)} %get-tuple-element.56), channel_id=1, source_target_pairs={{1,0},{2,1},{3,2},{4,3},{5,4},{6,5},{7,6},{8,7},{9,8},{10,9},{11,1... | collective-permute-start | bytes 589832 | tf_op jit(solution)/shard_map/ppermute | solution.py:29
  7.9 4.8 %collective-permute-start.1 = (bf16[192,512]{1,0:T(8,128)(2,1)}, bf16[192,512]{1,0:T(8,128)(2,1)S(1)}, u32[]{:S(2)}, u32[]{:S(2)}) collective-permute-start(bf16[192,512]{1,0:T(8,128)(2,1)} %get-tuple-element.57), channel_id=1, source_target_pairs={{32,0},{64,32},{96,64},{128,96},{160,128},{192,160},{224,192},{0,2... | collective-permute-start | bytes 589832 | tf_op jit(solution)/shard_map/ppermute | solution.py:31
  12.7 0.7 multiply_add_fusion
  13.5 0.7 reshape.52.place_ref.refs_0_
  14.2 3.9 %collective-permute-done.1.refs_2_.refs_1_ = bf16[192,512]{1,0:T(8,128)(2,1)S(1)} collective-permute-done((bf16[192,512]{1,0:T(8,128)(2,1)}, bf16[192,512]{1,0:T(8,128)(2,1)S(1)}, u32[]{:S(2)}, u32[]{:S(2)}) %collective-permute-start.1) | collective-permute-done | bytes 196640 | tf_op jit(solution)/shard_map/ppermute | solution.py:31
  18.1 0.7 copy-done.15
  18.7 0.7 copy-done.16
  19.4 2.9 %to_slots.1 = (bf16[512,512]{1,0:T(8,128)(2,1)}, bf16[256,512]{1,0:T(8,128)(2,1)}, bf16[256,512]{1,0:T(8,128)(2,1)}) custom-call(s32[1,256]{1,0:T(1,128)} %reshape.52.place_ref.refs_0_, bf16[16,16,512]{2,1,0:T(8,128)(2,1)} %cot_hbm.1, bf16[16,16,512]{2,1,0:T(8,128)(2,1)} %residual_hbm.1, bf16[192,512]{1,0:T(8,128)(2,1)} %copy-done.14, ...), custom_call_target="tpu_custom_call" | custom-call | tf_op jit(solution)/shard_map/to_slots/pallas_call | solution.py:484
  22.4 7.7 %all-to-all-start.1 = ((bf16[32,16,512]{2,1,0:T(8,128)(2,1)}), bf16[32,16,512]{2,1,0:T(8,128)(2,1)S(1)}, u32[]{:S(2)}, u32[]{:S(2)}) async-start(bf16[32,16,512]{2,1,0:T(8,128)(2,1)} %bitcast.39), calls=%async_computation.1 | async-start | bytes 1048576 | tf_op jit(solution)/shard_map/all_to_all | solution.py:658
  30.1 8.0 %attend.1 = (bf16[64,512]{1,0:T(8,128)(2,1)}, bf16[64,512]{1,0:T(8,128)(2,1)}, bf16[64,512]{1,0:T(8,128)(2,1)}, bf16[64,512]{1,0:T(8,128)(2,1)}, bf16[16,256,256]{2,1,0:T(8,128)(2,1)}) custom-call(s32[1]{0:T(128)} %bitcast.2.last_ref, bf16[192,512]{1,0:T(8,128)(2,1)} %get-tuple-element.55.refs_0_, bf16[192,512]{1,0:T(8,128)(2,1)} %copy-done.14, ...), custom_call_target="tpu_custom_call" | custom-call | flops 536870912 | bytes 1572864 | tf_op jit(solution)/shard_map/attend/pallas_call | solution.py:166
  38.0 0.9 collective-permute-start.4
  38.9 1.0 collective-permute-start.5
  39.9 10.2 %collective-permute-done.3.refs_3_.refs_6_ = bf16[64,512]{1,0:T(8,128)(2,1)S(1)} collective-permute-done((bf16[64,512]{1,0:T(8,128)(2,1)}, bf16[64,512]{1,0:T(8,128)(2,1)S(1)}, u32[]{:S(2)}, u32[]{:S(2)}) %collective-permute-start.3) | collective-permute-done | bytes 65568 | tf_op jit(solution)/shard_map/ppermute | solution.py:37
  50.2 0.6 copy-done.11
  50.8 2.8 %norm.1 = (bf16[512,512]{1,0:T(8,128)(2,1)}, f32[256,512]{1,0:T(8,128)}, f32[256,1]{1,0:T(8,128)}) custom-call(s32[1,256]{1,0:T(1,128)} %reshape.52.place_ref.refs_0_, f32[1,512]{1,0:T(1,128)} %bitcast.42, bf16[512,512]{1,0:T(8,128)(2,1)} %refs_2_.5, bf16[64,512]{1,0:T(8,128)(2,1)} %copy-done.11, bf16[64,512]{1,0:T(8,128)(2,1)} %copy-done.12, ...), custom_call_target="tpu_custom_call" | custom-call | bytes 1 | tf_op jit(solution)/shard_map/norm/pallas_call | solution.py:147
  53.7 7.5 %all-to-all-start = ((bf16[32,16,512]{2,1,0:T(8,128)(2,1)}), bf16[32,16,512]{2,1,0:T(8,128)(2,1)S(1)}, u32[]{:S(2)}, u32[]{:S(2)}) async-start(bf16[32,16,512]{2,1,0:T(8,128)(2,1)} %bitcast.37), calls=%async_computation | async-start | bytes 1048576 | tf_op jit(solution)/shard_map/all_to_all | solution.py:658
  61.3 1.3 collective-permute-start.6
  62.6 0.7 convert_bitcast_fusion
  63.3 0.6 reshape.60.router_hbm.refs_4_
  63.9 0.6 pad_add_fusion.units_ref
  64.5 13.9 %all-to-all-done = bf16[32,16,512]{2,1,0:T(8,128)(2,1)S(1)} async-done(((bf16[32,16,512]{2,1,0:T(8,128)(2,1)}), bf16[32,16,512]{2,1,0:T(8,128)(2,1)S(1)}, u32[]{:S(2)}, u32[]{:S(2)}) %all-to-all-start) | async-done | bytes 524320 | tf_op jit(solution)/shard_map/all_to_all | solution.py:658
  78.4 1.5 collective-permute-start.7
  79.9 1.7 collective-permute-done.6.refs_0_.refs_3_
  81.7 0.8 copy-done.24
  82.5 11.3 %experts.1 = (bf16[2,256,512]{2,1,0:T(8,128)(2,1)}, f32[2,2,512]{2,1,0:T(2,128)}) custom-call(bf16[2,256,512]{2,1,0:T(8,128)(2,1)} %copy-done.10, bf16[2,256,512]{2,1,0:T(8,128)(2,1)} %copy-done.9, f32[2,1,512]{2,1,0:T(1,128)} %reshape.60.router_hbm.refs_4_, f32[1,512]{1,0:T(1,128)} %bitcast.43, bf16[2,512,2048]{2,1,0:T(8,128)(2,1)} %refs_5_.1, ...), custom_call_target="tpu_custom_call" | custom-call | flops 6442450944 | bytes 8388608 | tf_op jit(solution)/shard_map/experts/pallas_call | solution.py:256
  93.8 0.8 copy-done.8
  94.7 1.9 to_devices.1
  96.5 7.8 %all-to-all-start.2 = ((bf16[32,16,512]{2,1,0:T(8,128)(2,1)}), bf16[32,16,512]{2,1,0:T(8,128)(2,1)S(1)}, u32[]{:S(2)}, u32[]{:S(2)}) async-start(bf16[32,16,512]{2,1,0:T(8,128)(2,1)} %to_devices.1), calls=%async_computation.2 | async-start | bytes 1048576 | tf_op jit(solution)/shard_map/all_to_all | solution.py:681
  104.4 12.6 %weight_sums.1 = (bf16[2,512,256]{2,1,0:T(8,128)(2,1)}, bf16[2,512,256]{2,1,0:T(8,128)(2,1)}, bf16[2,2,512,256]{3,2,1,0:T(8,128)(2,1)}, bf16[2,2,512,256]{3,2,1,...) custom-call(s32[4]{0:T(128)} %pad_add_fusion.units_ref, bf16[2,256,512]{2,1,0:T(8,128)(2,1)} %copy-done.10, ...), custom_call_target="tpu_custom_call" | custom-call | flops 8589934592 | bytes 4194304 | tf_op jit(solution)/shard_map/weight_sums/pallas_call | solution.py:331
  117.1 3.2 %collective-permute-start.15 = (bf16[2,512,256]{2,1,0:T(8,128)(2,1)}, bf16[2,512,256]{2,1,0:T(8,128)(2,1)S(1)}, u32[]{:S(2)}, u32[]{:S(2)}) collective-permute-start(bf16[2,512,256]{2,1,0:T(8,128)(2,1)} %get-tuple-element.92), channel_id=1, source_target_pairs={{0,96},{32,0},{64,32},{96,64},{1,97},{33,1},{65,33},{97,65},{2,98}... | collective-permute-start | bytes 1572872 | tf_op jit(solution)/shard_map/ppermute | solution.py:46
  120.3 1.2 all-to-all-done.2
  121.6 0.8 copy-done.3
  122.4 3.3 %token_grads.1 = (bf16[64,512]{1,0:T(8,128)(2,1)}, bf16[64,512]{1,0:T(8,128)(2,1)}, bf16[64,512]{1,0:T(8,128)(2,1)}, bf16[64,512]{1,0:T(8,128)(2,1)}, bf16[64,51...) custom-call(s32[1,256]{1,0:T(1,128)} %reshape.52.place_ref.refs_0_, ...), custom_call_target="tpu_custom_call" | custom-call | bytes 1 | tf_op jit(solution)/shard_map/token_grads/pallas_call | solution.py:147
  125.7 7.1 %all-to-all-start.3 = ((bf16[32,16,512]{2,1,0:T(8,128)(2,1)}), bf16[32,16,512]{2,1,0:T(8,128)(2,1)S(1)}, u32[]{:S(2)}, u32[]{:S(2)}) async-start(bf16[32,16,512]{2,1,0:T(8,128)(2,1)} %bitcast.38), calls=%async_computation.3 | async-start | bytes 1048576 | tf_op jit(solution)/shard_map/all_to_all | solution.py:702
  132.8 2.5 %collective-permute-start.8 = (bf16[64,512]{1,0:T(8,128)(2,1)}, bf16[64,512]{1,0:T(8,128)(2,1)S(1)}, u32[]{:S(2)}, u32[]{:S(2)}) collective-permute-start(bf16[64,512]{1,0:T(8,128)(2,1)} %get-tuple-element.73), channel_id=1, source_target_pairs={{1,0},{2,1},{3,2},{4,3},{5,4},{6,5},{7,6},{8,7},{9,8},{10,9},{11,1... | collective-permute-start | bytes 196616 | tf_op jit(solution)/shard_map/ppermute | solution.py:29
  135.3 1.2 collective-permute-start.9
  136.6 7.9 %collective-permute-done.8.refs_5_.refs_4_ = bf16[64,512]{1,0:T(8,128)(2,1)S(1)} collective-permute-done((bf16[64,512]{1,0:T(8,128)(2,1)}, bf16[64,512]{1,0:T(8,128)(2,1)S(1)}, u32[]{:S(2)}, u32[]{:S(2)}) %collective-permute-start.8) | collective-permute-done | bytes 65568 | tf_op jit(solution)/shard_map/ppermute | solution.py:29
  144.5 1.7 collective-permute-done.10.refs_7_.refs_6_
  146.2 0.6 copy-done.22
  146.8 3.4 %join.1 = (bf16[2,2,512,256]{3,2,1,0:T(8,128)(2,1)}, bf16[2,2,512,256]{3,2,1,0:T(8,128)(2,1)}) custom-call(bf16[2,2,512,256]{3,2,1,0:T(8,128)(2,1)} %get-tuple-element.89.refs_0_, bf16[2,2,512,256]{3,2,1,0:T(8,128)(2,1)} %get-tuple-element.90.refs_1_, bf16[2,512,256]{2,1,0:T(8,128)(2,1)} %copy-done.6, bf16[2,512,256]{2,1,0:T(8,128)(2,1)} %copy-done.7, ...), custom_call_target="tpu_custom_call" | custom-call | bytes 1 | tf_op jit(solution)/shard_map/join/pallas_call | solution.py:147
  150.5 3.2 %collective-permute-start.17 = (bf16[2,2,512,256]{3,2,1,0:T(8,128)(2,1)}, bf16[2,2,512,256]{3,2,1,0:T(8,128)(2,1)S(1)}, u32[]{:S(2)}, u32[]{:S(2)}) collective-permute-start(bf16[2,2,512,256]{3,2,1,0:T(8,128)(2,1)} %get-tuple-element.94), channel_id=1, source_target_pairs={{0,96},{32,0},{64,32},{96,64},{1,97},{33,1},{65,33},{97,65},{2,98}... | collective-permute-start | bytes 3145736 | tf_op jit(solution)/shard_map/ppermute | solution.py:46
  153.8 0.6 select_maximum_fusion.refs_1_
  154.4 6.4 %attend_back.1 = (bf16[192,512]{1,0:T(8,128)(2,1)}, bf16[192,512]{1,0:T(8,128)(2,1)}, bf16[192,512]{1,0:T(8,128)(2,1)}, bf16[192,512]{1,0:T(8,128)(2,1)}) custom-call(bf16[192,512]{1,0:T(8,128)(2,1)} %get-tuple-element.55.refs_0_, bf16[192,512]{1,0:T(8,128)(2,1)} %copy-done.14, bf16[192,512]{1,0:T(8,128)(2,1)} %copy-done.15, bf16[192,512]{1,0:T(8,128)(2,1)} %copy-done.16, ...), custom_call_target="tpu_custom_call" | custom-call | flops 1073741824 | bytes 3145728 | tf_op jit(solution)/shard_map/attend_back/pallas_call | solution.py:186
  160.8 0.8 copy-done.4
  161.6 1.8 share_sum.2
  163.4 3.4 %all-to-all-start.4 = ((bf16[8,24,512]{2,1,0:T(8,128)(2,1)}), bf16[8,24,512]{2,1,0:T(8,128)(2,1)S(1)}, u32[]{:S(2)}, u32[]{:S(2)}) async-start(bf16[8,24,512]{2,1,0:T(8,128)(2,1)} %share_sum.2), calls=%async_computation.4 | async-start | bytes 393216 | tf_op jit(solution)/shard_map/all_to_all | solution.py:703
  166.9 10.0 %collective-permute-done.16.refs_1_.up_ref = bf16[2,2,512,256]{3,2,1,0:T(8,128)(2,1)S(1)} collective-permute-done((bf16[2,2,512,256]{3,2,1,0:T(8,128)(2,1)}, bf16[2,2,512,256]{3,2,1,0:T(8,128)(2,1)S(1)}, u32[]{:S(2)}, u32[]{:S(2)}) %collective-permute-start.16) | collective-permute-done | bytes 1048608 | tf_op jit(solution)/shard_map/ppermute | solution.py:46
  176.9 2.9 %all-to-all-done.4.refs_0_ = bf16[8,24,512]{2,1,0:T(8,128)(2,1)S(1)} async-done(((bf16[8,24,512]{2,1,0:T(8,128)(2,1)}), bf16[8,24,512]{2,1,0:T(8,128)(2,1)S(1)}, u32[]{:S(2)}, u32[]{:S(2)}) %all-to-all-start.4) | async-done | bytes 196640 | tf_op jit(solution)/shard_map/all_to_all | solution.py:703
  179.7 0.7 copy-done.5
  180.4 1.9 share_sum.3
  182.3 9.5 %all-to-all-start.5 = ((bf16[32,24,512]{2,1,0:T(8,128)(2,1)}), bf16[32,24,512]{2,1,0:T(8,128)(2,1)S(1)}, u32[]{:S(2)}, u32[]{:S(2)}) async-start(bf16[32,24,512]{2,1,0:T(8,128)(2,1)} %share_sum.3), calls=%async_computation.5 | async-start | bytes 1572864 | tf_op jit(solution)/shard_map/all_to_all | solution.py:704
  191.8 0.5 collective-permute-start.11
  192.7 1.0 collective-permute-start.13
  193.7 2.8 %tiles.3 = bf16[16,16,512]{2,1,0:T(8,128)(2,1)} custom-call(bf16[64,512]{1,0:T(8,128)(2,1)} %get-tuple-element.84.refs_0_, bf16[64,512]{1,0:T(8,128)(2,1)} %get-tuple-element.85.refs_1_, bf16[64,512]{1,0:T(8,128)(2,1)} %get-tuple-element.86.refs_2_, bf16[64,512]{1,0:T(8,128)(2,1)} %get-tuple-element.87.refs_3_), custom_call_target="tpu_custom_call" | custom-call | tf_op jit(solution)/shard_map/tiles/pallas_call | solution.py:446
  196.5 20.5 %collective-permute-done.11.refs_0_ = bf16[192,512]{1,0:T(8,128)(2,1)S(1)} collective-permute-done((bf16[192,512]{1,0:T(8,128)(2,1)S(1)}, bf16[192,512]{1,0:T(8,128)(2,1)S(1)}, u32[]{:S(2)}, u32[]{:S(2)}) %collective-permute-start.11) | collective-permute-done | bytes 196640 | tf_op jit(solution)/shard_map/ppermute | solution.py:37
  217.1 0.7 copy-done.17
  217.8 0.7 copy-done.19
  218.5 3.2 %tiles.2 = (bf16[16,16,512]{2,1,0:T(8,128)(2,1)}, bf16[16,16,512]{2,1,0:T(8,128)(2,1)}, bf16[16,16,512]{2,1,0:T(8,128)(2,1)}) custom-call(bf16[192,512]{1,0:T(8,128)(2,1)} %copy-done.17, bf16[192,512]{1,0:T(8,128)(2,1)} %copy-done.18, bf16[192,512]{1,0:T(8,128)(2,1)} %copy-done.19, bf16[192,512]{1,0:T(8,128)(2,1)} %get-tuple-element.80.refs_3_.refs_2_), custom_call_target="tpu_custom_call" | custom-call | tf_op jit(solution)/shard_map/tiles/pallas_call | solution.py:446
  221.7 3.1 %weight_total.1 = (bf16[2,512,256]{2,1,0:T(8,128)(2,1)}, bf16[2,256,512]{2,1,0:T(8,128)(2,1)}) custom-call(f32[2,2,512,256]{3,2,1,0:T(8,128)} %get-tuple-element.98.own_ref, bf16[2,2,512,256]{3,2,1,0:T(8,128)(2,1)} %copy-done, bf16[2,2,512,256]{3,2,1,0:T(8,128)(2,1)} %copy-done.1), custom_call_target="tpu_custom_call" | custom-call | tf_op jit(solution)/shard_map/weight_total/pallas_call | solution.py:381
  224.8 0.9 copy-done.2
  225.7 2.2 finish.1
  228.0 1.1 slice.11
  229.0 0.7 reshape.59
  (71 shorter events, 1.3 us)
Async XLA Ops:
  2.7 11.5 %collective-permute-start = (bf16[192,512]{1,0:T(8,128)(2,1)}, bf16[192,512]{1,0:T(8,128)(2,1)S(1)}, u32[]{:S(2)}, u32[]{:S(2)}) collective-permute-start(bf16[192,512]{1,0:T(8,128)(2,1)} %get-tuple-element.56), channel_id=1, source_target_pairs={{1,0},{2,1},{3,2},{4,3},{5,4},{6,5},{7,6},{8,7},{9,8},{10,9},{11,1... | collective-permute-start | bytes 589832 | tf_op jit(solution)/shard_map/ppermute | solution.py:29
  7.9 10.1 %collective-permute-start.1 = (bf16[192,512]{1,0:T(8,128)(2,1)}, bf16[192,512]{1,0:T(8,128)(2,1)S(1)}, u32[]{:S(2)}, u32[]{:S(2)}) collective-permute-start(bf16[192,512]{1,0:T(8,128)(2,1)} %get-tuple-element.57), channel_id=1, source_target_pairs={{32,0},{64,32},{96,64},{128,96},{160,128},{192,160},{224,192},{0,2... | collective-permute-start | bytes 589832 | tf_op jit(solution)/shard_map/ppermute | solution.py:31
  12.7 5.4 %collective-permute-start.2 = (bf16[192,512]{1,0:T(8,128)(2,1)}, bf16[192,512]{1,0:T(8,128)(2,1)S(1)}, u32[]{:S(2)}, u32[]{:S(2)}) collective-permute-start(bf16[192,512]{1,0:T(8,128)(2,1)} %get-tuple-element.58), channel_id=1, source_target_pairs={{33,0},{34,1},{35,2},{36,3},{37,4},{38,5},{39,6},{40,7},{41,8},{42... | collective-permute-start | bytes 589832 | tf_op jit(solution)/shard_map/ppermute | solution.py:37
  14.2 3.9 %copy-start.14 = (bf16[192,512]{1,0:T(8,128)(2,1)}, bf16[192,512]{1,0:T(8,128)(2,1)S(1)}, u32[]{:S(2)}) copy-start(bf16[192,512]{1,0:T(8,128)(2,1)S(1)} %collective-permute-done.refs_1_.refs_0_) | copy-start | bytes 589828
  18.1 0.7 copy-start.15
  18.7 0.7 copy-start.16
  22.4 31.3 %all-to-all-start.1 = ((bf16[32,16,512]{2,1,0:T(8,128)(2,1)}), bf16[32,16,512]{2,1,0:T(8,128)(2,1)S(1)}, u32[]{:S(2)}, u32[]{:S(2)}) async-start(bf16[32,16,512]{2,1,0:T(8,128)(2,1)} %bitcast.39), calls=%async_computation.1 | async-start | bytes 1048576 | tf_op jit(solution)/shard_map/all_to_all | solution.py:658
  38.0 12.1 %collective-permute-start.3 = (bf16[64,512]{1,0:T(8,128)(2,1)}, bf16[64,512]{1,0:T(8,128)(2,1)S(1)}, u32[]{:S(2)}, u32[]{:S(2)}) collective-permute-start(bf16[64,512]{1,0:T(8,128)(2,1)} %get-tuple-element.59), channel_id=1, source_target_pairs={{255,0},{224,1},{225,2},{226,3},{227,4},{228,5},{229,6},{230,7},{2... | collective-permute-start | bytes 196616 | tf_op jit(solution)/shard_map/ppermute | solution.py:37
  38.0 12.1 %collective-permute-start.4 = (bf16[64,512]{1,0:T(8,128)(2,1)}, bf16[64,512]{1,0:T(8,128)(2,1)S(1)}, u32[]{:S(2)}, u32[]{:S(2)}) collective-permute-start(bf16[64,512]{1,0:T(8,128)(2,1)} %get-tuple-element.60), channel_id=1, source_target_pairs={{224,0},{0,32},{32,64},{64,96},{96,128},{128,160},{160,192},{192,2... | collective-permute-start | bytes 196616 | tf_op jit(solution)/shard_map/ppermute | solution.py:31
  38.9 11.2 %collective-permute-start.5 = (bf16[64,512]{1,0:T(8,128)(2,1)}, bf16[64,512]{1,0:T(8,128)(2,1)S(1)}, u32[]{:S(2)}, u32[]{:S(2)}) collective-permute-start(bf16[64,512]{1,0:T(8,128)(2,1)} %get-tuple-element.61), channel_id=1, source_target_pairs={{31,0},{0,1},{1,2},{2,3},{3,4},{4,5},{5,6},{6,7},{7,8},{8,9},{9,10... | collective-permute-start | bytes 196616 | tf_op jit(solution)/shard_map/ppermute | solution.py:29
  50.1 0.6 copy-start.11
  50.2 0.6 copy-start.12
  50.2 0.7 copy-start.13
  53.7 24.7 %all-to-all-start = ((bf16[32,16,512]{2,1,0:T(8,128)(2,1)}), bf16[32,16,512]{2,1,0:T(8,128)(2,1)S(1)}, u32[]{:S(2)}, u32[]{:S(2)}) async-start(bf16[32,16,512]{2,1,0:T(8,128)(2,1)} %bitcast.37), calls=%async_computation | async-start | bytes 1048576 | tf_op jit(solution)/shard_map/all_to_all | solution.py:658
  61.2 20.4 %copy-start.9 = (bf16[2,256,512]{2,1,0:T(8,128)(2,1)}, bf16[2,256,512]{2,1,0:T(8,128)(2,1)S(1)}, u32[]{:S(2)}) copy-start(bf16[2,256,512]{2,1,0:T(8,128)(2,1)S(1)} %copy_bitcast_fusion.cot_hbm.refs_2_) | copy-start | bytes 1572868
  61.3 20.4 %collective-permute-start.6 = (bf16[2,256,512]{2,1,0:T(8,128)(2,1)S(1)}, bf16[2,256,512]{2,1,0:T(8,128)(2,1)S(1)}, u32[]{:S(2)}, u32[]{:S(2)}) collective-permute-start(bf16[2,256,512]{2,1,0:T(8,128)(2,1)S(1)} %copy_bitcast_fusion.cot_hbm.refs_2_), channel_id=1, source_target_pairs={{0,128},{128,0},{1,129},{129,1},{2,130},{130,2},{3,131},{131,3},{4... | collective-permute-start | bytes 1572872 | tf_op jit(solution)/shard_map/ppermute | solution.py:41
  78.4 3.3 %copy-start.10 = (bf16[2,256,512]{2,1,0:T(8,128)(2,1)}, bf16[2,256,512]{2,1,0:T(8,128)(2,1)S(1)}, u32[]{:S(2)}) copy-start(bf16[2,256,512]{2,1,0:T(8,128)(2,1)S(1)} %copy_bitcast_fusion.1.hidden_hbm.refs_0_) | copy-start | bytes 1572868
  78.4 15.4 %collective-permute-start.7 = (bf16[2,256,512]{2,1,0:T(8,128)(2,1)S(1)}, bf16[2,256,512]{2,1,0:T(8,128)(2,1)S(1)}, u32[]{:S(2)}, u32[]{:S(2)}) collective-permute-start(bf16[2,256,512]{2,1,0:T(8,128)(2,1)S(1)} %copy_bitcast_fusion.1.hidden_hbm.refs_0_), channel_id=1, source_target_pairs={{0,128},{128,0},{1,129},{129,1},{2,130},{130,2},{3,131},{131,3},{4... | collective-permute-start | bytes 1572872 | tf_op jit(solution)/shard_map/ppermute | solution.py:41
  81.7 0.8 copy-start.24
  93.8 0.8 copy-start.8
  96.5 25.0 %all-to-all-start.2 = ((bf16[32,16,512]{2,1,0:T(8,128)(2,1)}), bf16[32,16,512]{2,1,0:T(8,128)(2,1)S(1)}, u32[]{:S(2)}, u32[]{:S(2)}) async-start(bf16[32,16,512]{2,1,0:T(8,128)(2,1)} %to_devices.1), calls=%async_computation.2 | async-start | bytes 1048576 | tf_op jit(solution)/shard_map/all_to_all | solution.py:681
  117.0 36.8 %copy-start.23 = (f32[2,2,512]{2,1,0:T(2,128)S(1)}, f32[2,2,512]{2,1,0:T(2,128)}, u32[]{:S(2)}) copy-start(f32[2,2,512]{2,1,0:T(2,128)} %get-tuple-element.70.refs_7_) | copy-start | bytes 24580
  117.0 19.5 %collective-permute-start.14 = (bf16[2,512,256]{2,1,0:T(8,128)(2,1)}, bf16[2,512,256]{2,1,0:T(8,128)(2,1)S(1)}, u32[]{:S(2)}, u32[]{:S(2)}) collective-permute-start(bf16[2,512,256]{2,1,0:T(8,128)(2,1)} %get-tuple-element.91), channel_id=1, source_target_pairs={{0,32},{32,64},{64,96},{96,0},{1,33},{33,65},{65,97},{97,1},{2,34}... | collective-permute-start | bytes 1572872 | tf_op jit(solution)/shard_map/ppermute | solution.py:46
  117.1 19.4 %collective-permute-start.15 = (bf16[2,512,256]{2,1,0:T(8,128)(2,1)}, bf16[2,512,256]{2,1,0:T(8,128)(2,1)S(1)}, u32[]{:S(2)}, u32[]{:S(2)}) collective-permute-start(bf16[2,512,256]{2,1,0:T(8,128)(2,1)} %get-tuple-element.92), channel_id=1, source_target_pairs={{0,96},{32,0},{64,32},{96,64},{1,97},{33,1},{65,33},{97,65},{2,98}... | collective-permute-start | bytes 1572872 | tf_op jit(solution)/shard_map/ppermute | solution.py:46
  121.6 0.8 copy-start.3
  125.7 35.1 %all-to-all-start.3 = ((bf16[32,16,512]{2,1,0:T(8,128)(2,1)}), bf16[32,16,512]{2,1,0:T(8,128)(2,1)S(1)}, u32[]{:S(2)}, u32[]{:S(2)}) async-start(bf16[32,16,512]{2,1,0:T(8,128)(2,1)} %bitcast.38), calls=%async_computation.3 | async-start | bytes 1048576 | tf_op jit(solution)/shard_map/all_to_all | solution.py:702
  132.8 11.7 %collective-permute-start.8 = (bf16[64,512]{1,0:T(8,128)(2,1)}, bf16[64,512]{1,0:T(8,128)(2,1)S(1)}, u32[]{:S(2)}, u32[]{:S(2)}) collective-permute-start(bf16[64,512]{1,0:T(8,128)(2,1)} %get-tuple-element.73), channel_id=1, source_target_pairs={{1,0},{2,1},{3,2},{4,3},{5,4},{6,5},{7,6},{8,7},{9,8},{10,9},{11,1... | collective-permute-start | bytes 196616 | tf_op jit(solution)/shard_map/ppermute | solution.py:29
  135.3 9.2 %collective-permute-start.9 = (bf16[64,512]{1,0:T(8,128)(2,1)}, bf16[64,512]{1,0:T(8,128)(2,1)S(1)}, u32[]{:S(2)}, u32[]{:S(2)}) collective-permute-start(bf16[64,512]{1,0:T(8,128)(2,1)} %get-tuple-element.74), channel_id=1, source_target_pairs={{32,0},{64,32},{96,64},{128,96},{160,128},{192,160},{224,192},{0,2... | collective-permute-start | bytes 196616 | tf_op jit(solution)/shard_map/ppermute | solution.py:31
  136.5 9.7 %collective-permute-start.10 = (bf16[64,512]{1,0:T(8,128)(2,1)}, bf16[64,512]{1,0:T(8,128)(2,1)S(1)}, u32[]{:S(2)}, u32[]{:S(2)}) collective-permute-start(bf16[64,512]{1,0:T(8,128)(2,1)} %get-tuple-element.75), channel_id=1, source_target_pairs={{33,0},{34,1},{35,2},{36,3},{37,4},{38,5},{39,6},{40,7},{41,8},{42... | collective-permute-start | bytes 196616 | tf_op jit(solution)/shard_map/ppermute | solution.py:37
  136.5 9.7 %copy-start.6 = (bf16[2,512,256]{2,1,0:T(8,128)(2,1)}, bf16[2,512,256]{2,1,0:T(8,128)(2,1)S(1)}, u32[]{:S(2)}) copy-start(bf16[2,512,256]{2,1,0:T(8,128)(2,1)S(1)} %collective-permute-done.14.refs_2_) | copy-start | bytes 1572868
  136.5 9.7 %copy-start.7 = (bf16[2,512,256]{2,1,0:T(8,128)(2,1)}, bf16[2,512,256]{2,1,0:T(8,128)(2,1)S(1)}, u32[]{:S(2)}) copy-start(bf16[2,512,256]{2,1,0:T(8,128)(2,1)S(1)} %collective-permute-done.15.refs_3_) | copy-start | bytes 1572868
  144.5 1.7 copy-start.20
  144.5 1.7 copy-start.21
  146.2 0.6 copy-start.22
  150.2 26.7 %collective-permute-start.16 = (bf16[2,2,512,256]{3,2,1,0:T(8,128)(2,1)}, bf16[2,2,512,256]{3,2,1,0:T(8,128)(2,1)S(1)}, u32[]{:S(2)}, u32[]{:S(2)}) collective-permute-start(bf16[2,2,512,256]{3,2,1,0:T(8,128)(2,1)} %get-tuple-element.93.refs_3_), channel_id=1, source_target_pairs={{0,32},{32,64},{64,96},{96,0},{1,33},{33,65},{65,97},{97,1},{2,34}... | collective-permute-start | bytes 3145736 | tf_op jit(solution)/shard_map/ppermute | solution.py:46
  150.5 26.3 %collective-permute-start.17 = (bf16[2,2,512,256]{3,2,1,0:T(8,128)(2,1)}, bf16[2,2,512,256]{3,2,1,0:T(8,128)(2,1)S(1)}, u32[]{:S(2)}, u32[]{:S(2)}) collective-permute-start(bf16[2,2,512,256]{3,2,1,0:T(8,128)(2,1)} %get-tuple-element.94), channel_id=1, source_target_pairs={{0,96},{32,0},{64,32},{96,64},{1,97},{33,1},{65,33},{97,65},{2,98}... | collective-permute-start | bytes 3145736 | tf_op jit(solution)/shard_map/ppermute | solution.py:46
  160.8 31.1 %copy-start.27 = (bf16[192,512]{1,0:T(8,128)(2,1)S(1)}, bf16[192,512]{1,0:T(8,128)(2,1)}, u32[]{:S(2)}) copy-start(bf16[192,512]{1,0:T(8,128)(2,1)} %get-tuple-element.77) | copy-start | bytes 589828
  160.8 31.6 %copy-start.26 = (bf16[192,512]{1,0:T(8,128)(2,1)S(1)}, bf16[192,512]{1,0:T(8,128)(2,1)}, u32[]{:S(2)}) copy-start(bf16[192,512]{1,0:T(8,128)(2,1)} %get-tuple-element.78) | copy-start | bytes 589828
  160.8 31.9 %copy-start.25 = (bf16[192,512]{1,0:T(8,128)(2,1)S(1)}, bf16[192,512]{1,0:T(8,128)(2,1)}, u32[]{:S(2)}) copy-start(bf16[192,512]{1,0:T(8,128)(2,1)} %get-tuple-element.79) | copy-start | bytes 589828
  160.8 0.8 copy-start.4
  163.4 16.3 %all-to-all-start.4 = ((bf16[8,24,512]{2,1,0:T(8,128)(2,1)}), bf16[8,24,512]{2,1,0:T(8,128)(2,1)S(1)}, u32[]{:S(2)}, u32[]{:S(2)}) async-start(bf16[8,24,512]{2,1,0:T(8,128)(2,1)} %share_sum.2), calls=%async_computation.4 | async-start | bytes 393216 | tf_op jit(solution)/shard_map/all_to_all | solution.py:703
  176.8 2.9 %copy-start = (bf16[2,2,512,256]{3,2,1,0:T(8,128)(2,1)}, bf16[2,2,512,256]{3,2,1,0:T(8,128)(2,1)S(1)}, u32[]{:S(2)}) copy-start(bf16[2,2,512,256]{3,2,1,0:T(8,128)(2,1)S(1)} %collective-permute-done.16.refs_1_.up_ref) | copy-start | bytes 3145732
  176.8 2.9 %copy-start.1 = (bf16[2,2,512,256]{3,2,1,0:T(8,128)(2,1)}, bf16[2,2,512,256]{3,2,1,0:T(8,128)(2,1)S(1)}, u32[]{:S(2)}) copy-start(bf16[2,2,512,256]{3,2,1,0:T(8,128)(2,1)S(1)} %collective-permute-done.17.refs_2_.down_ref) | copy-start | bytes 3145732
  179.7 0.7 copy-start.5
  182.3 42.5 %all-to-all-start.5 = ((bf16[32,24,512]{2,1,0:T(8,128)(2,1)}), bf16[32,24,512]{2,1,0:T(8,128)(2,1)S(1)}, u32[]{:S(2)}, u32[]{:S(2)}) async-start(bf16[32,24,512]{2,1,0:T(8,128)(2,1)} %share_sum.3), calls=%async_computation.5 | async-start | bytes 1572864 | tf_op jit(solution)/shard_map/all_to_all | solution.py:704
  191.8 25.2 %collective-permute-start.11 = (bf16[192,512]{1,0:T(8,128)(2,1)S(1)}, bf16[192,512]{1,0:T(8,128)(2,1)S(1)}, u32[]{:S(2)}, u32[]{:S(2)}) collective-permute-start(bf16[192,512]{1,0:T(8,128)(2,1)S(1)} %copy-done.27), channel_id=1, source_target_pairs={{255,0},{224,1},{225,2},{226,3},{227,4},{228,5},{229,6},{230,7},{2... | collective-permute-start | bytes 589832 | tf_op jit(solution)/shard_map/ppermute | solution.py:37
  192.4 24.7 %collective-permute-start.12 = (bf16[192,512]{1,0:T(8,128)(2,1)S(1)}, bf16[192,512]{1,0:T(8,128)(2,1)S(1)}, u32[]{:S(2)}, u32[]{:S(2)}) collective-permute-start(bf16[192,512]{1,0:T(8,128)(2,1)S(1)} %copy-done.26), channel_id=1, source_target_pairs={{224,0},{0,32},{32,64},{64,96},{96,128},{128,160},{160,192},{192,2... | collective-permute-start | bytes 589832 | tf_op jit(solution)/shard_map/ppermute | solution.py:31
  192.7 24.4 %collective-permute-start.13 = (bf16[192,512]{1,0:T(8,128)(2,1)S(1)}, bf16[192,512]{1,0:T(8,128)(2,1)S(1)}, u32[]{:S(2)}, u32[]{:S(2)}) collective-permute-start(bf16[192,512]{1,0:T(8,128)(2,1)S(1)} %copy-done.25), channel_id=1, source_target_pairs={{31,0},{0,1},{1,2},{2,3},{3,4},{4,5},{5,6},{6,7},{7,8},{8,9},{9,10... | collective-permute-start | bytes 589832 | tf_op jit(solution)/shard_map/ppermute | solution.py:29
  217.1 0.7 copy-start.17
  217.1 0.7 copy-start.18
  217.8 0.7 copy-start.19
  224.8 0.9 copy-start.2
where the time goes:
time: 231 us; the launch traced here: 230 us
  waiting for transfers between devices  74.1 us (32%)
  starting transfers between devices  70.2 us (30%)
  Pallas kernels  69.6 us (30%)
  local copies, waits for them, and re-layouts  12.1 us (5%)
  other arithmetic  2.63 us (1%)
    ppermute x4, waiting for transfers between devices, fetch(): return lax.ppermute(block, EVERY, route)  32.5 us
    pallas_call x7, Pallas kernels, on_staged(): pl.pallas_call(functools.partial(staged, kernel, len(inputs)), in_specs=[...  17.4 us
    all_to_all x2, starting transfers between devices, exchange(): arrived = lax.all_to_all(slots, GX, 0, 0, tiled=True)  15.2 us
    all_to_all x2, waiting for transfers between devices, exchange(): arrived = lax.all_to_all(slots, GX, 0, 0, tiled=True)  13.9 us
    pallas_call x1, Pallas kernels, weight_sums(): pl.pallas_call(weights_kernel, in_specs=[SMEM] + [ANY] * (7 + len(earlier...  12.6 us
    pallas_call x1, Pallas kernels, experts(): pl.pallas_call(functools.partial(expert_kernel, chunk), in_specs=[ANY] *...  11.3 us
    ppermute x4, waiting for transfers between devices, step(): lax.ppermute(block, 'x', [(i, (i + way) % size) for i in range(size)])  10 us
    ppermute x4, starting transfers between devices, fetch(): lax.ppermute(block, GX, [((j + right) % cols, j) for j in range(cols)])  9.74 us
  transfers between devices with their start and end apart: 24, of which 10 were waited for; matrix products, arithmetic and copies ran while one was open for 2% of the time, Pallas kernels for 26%

commit v1 on v0

--- a/solution.py
+++ b/solution.py
@@ -697,12 +697,13 @@
 
     grads = attend_back(pieces, grad_mixed, probs, quarter, head_size, ())
 
+    image_out = tiles(window_to_image(grads), 3, side)
+
     extra = jnp.concatenate((small[:, 0], jnp.sum(small[:, 1], axis=0, keepdims=True)), axis=0)
     extra = jnp.pad(extra, ((0, -extra.shape[0] % 8), (0, 0)))
     shares = lax.all_to_all(proj_part.reshape(grid_cols, -1, width), GX, 0, 0, tiled=True)
     shares = lax.all_to_all(share_sum((shares, extra), grid_rows, (grads[0], upward)), GY, 0, 0, tiled=True)
-    summed = lax.all_to_all(share_sum((shares,), grid_cols, (from_below, from_above)), GX, 0, 0, tiled=True)
-    image_out = tiles(window_to_image(grads), 3, side)
+    summed = lax.all_to_all(share_sum((shares,), grid_cols, (from_below, from_above, image_out[0])), GX, 0, 0, tiled=True)
     grad_proj, grad_gain, further = finish(summed, width // grid_cols, local_experts, image_out[:1])
     grad_router = further[:, :local_experts].reshape(expert_count, width).T
     grad_in, grad_out = weight_total(own_sums, from_below, from_above)

time: 231 us -> 235 us (1.017)
  starting transfers between devices: 70.2 us -> 74 us
    all_to_all x1, waiting for transfers between devices: 0.01 us -> 16.4 us  [shards(): lax.all_to_all(share_sum((shares,), grid_cols, (from_below, from_above, i...]
    ppermute x4, waiting for transfers between devices: 32.5 us -> 18.6 us  [fetch(): return lax.ppermute(block, EVERY, route)]
    ppermute x4, waiting for transfers between devices: 10 us -> 0.01 us  [step(): lax.ppermute(block, 'x', [(i, (i + way) % size) for i in range(size)])]
    ppermute x4, waiting for transfers between devices: 3.89 us -> 12.9 us  [fetch(): lax.ppermute(block, GY, [((i + down) % rows, i) for i in range(rows)])]
    all_to_all x1, starting transfers between devices: 3.4 us -> 7.06 us  [shards(): lax.all_to_all(share_sum((shares, extra), grid_rows, (grads[0], upward)),...]
    all_to_all x1, waiting for transfers between devices: 2.85 us -> 0.01 us  [shards(): lax.all_to_all(share_sum((shares, extra), grid_rows, (grads[0], upward)),...]
    ppermute x4, starting transfers between devices: 7.25 us -> 9.96 us  [fetch(): lax.ppermute(block, GY, [((i + down) % rows, i) for i in range(rows)])]
    unnamed x56 -> x50, local copies, waits for them, and re-layouts: 8.9 us -> 9.5 us
  transfers between devices with their start and end apart: 24 -> 24, of which waited for: 10 -> 10; matrix products, arithmetic and copies ran while one was open for 2% -> 2% of each run, Pallas kernels for 26% -> 25%
where the time goes in v1:
time: 235 us; the launch traced here: 233 us
  starting transfers between devices  74 us (31%)
  waiting for transfers between devices  72.7 us (31%)
  Pallas kernels  69.7 us (30%)
  local copies, waits for them, and re-layouts  12.7 us (5%)
  other arithmetic  2.65 us (1%)
    ppermute x4, waiting for transfers between devices, fetch(): return lax.ppermute(block, EVERY, route)  18.6 us
    pallas_call x7, Pallas kernels, on_staged(): pl.pallas_call(functools.partial(staged, kernel, len(inputs)), in_specs=[...  17.3 us
    all_to_all x1, waiting for transfers between devices, shards(): lax.all_to_all(share_sum((shares,), grid_cols, (from_below, from_above, i...  16.4 us
    all_to_all x2, starting transfers between devices, exchange(): arrived = lax.all_to_all(slots, GX, 0, 0, tiled=True)  15.2 us
    all_to_all x2, waiting for transfers between devices, exchange(): arrived = lax.all_to_all(slots, GX, 0, 0, tiled=True)  13.9 us
    ppermute x4, waiting for transfers between devices, fetch(): lax.ppermute(block, GY, [((i + down) % rows, i) for i in range(rows)])  12.9 us
    pallas_call x1, Pallas kernels, weight_sums(): pl.pallas_call(weights_kernel, in_specs=[SMEM] + [ANY] * (7 + len(earlier...  12.6 us
    pallas_call x1, Pallas kernels, experts(): pl.pallas_call(functools.partial(expert_kernel, chunk), in_specs=[ANY] *...  11.3 us
  transfers between devices with their start and end apart: 24, of which 10 were waited for; matrix products, arithmetic and copies ran while one was open for 2% of the time, Pallas kernels for 25%

profile of v1, /device:TPU:8, one launch (start us, length us, event | category | flops | bytes accessed | tf_op | source)
XLA Modules:
  0.0 232.8 jit_solution(6068634042212949779)
XLA Ops:
  0.6 2.0 quarters.1
  2.7 5.3 %collective-permute-start = (bf16[192,512]{1,0:T(8,128)(2,1)}, bf16[192,512]{1,0:T(8,128)(2,1)S(1)}, u32[]{:S(2)}, u32[]{:S(2)}) collective-permute-start(bf16[192,512]{1,0:T(8,128)(2,1)} %get-tuple-element.56), channel_id=1, source_target_pairs={{1,0},{2,1},{3,2},{4,3},{5,4},{6,5},{7,6},{8,7},{9,8},{10,9},{11,1... | collective-permute-start | bytes 589832 | tf_op jit(solution)/shard_map/ppermute | solution.py:29
  7.9 4.8 %collective-permute-start.1 = (bf16[192,512]{1,0:T(8,128)(2,1)}, bf16[192,512]{1,0:T(8,128)(2,1)S(1)}, u32[]{:S(2)}, u32[]{:S(2)}) collective-permute-start(bf16[192,512]{1,0:T(8,128)(2,1)} %get-tuple-element.57), channel_id=1, source_target_pairs={{32,0},{64,32},{96,64},{128,96},{160,128},{192,160},{224,192},{0,2... | collective-permute-start | bytes 589832 | tf_op jit(solution)/shard_map/ppermute | solution.py:31
  12.7 0.7 multiply_add_fusion
  13.5 0.7 reshape.52.place_ref.refs_0_
  14.2 3.9 %collective-permute-done.1.refs_2_.refs_1_ = bf16[192,512]{1,0:T(8,128)(2,1)S(1)} collective-permute-done((bf16[192,512]{1,0:T(8,128)(2,1)}, bf16[192,512]{1,0:T(8,128)(2,1)S(1)}, u32[]{:S(2)}, u32[]{:S(2)}) %collective-permute-start.1) | collective-permute-done | bytes 196640 | tf_op jit(solution)/shard_map/ppermute | solution.py:31
  18.1 0.7 copy-done.15
  18.7 0.7 copy-done.16
  19.4 2.9 %to_slots.1 = (bf16[512,512]{1,0:T(8,128)(2,1)}, bf16[256,512]{1,0:T(8,128)(2,1)}, bf16[256,512]{1,0:T(8,128)(2,1)}) custom-call(s32[1,256]{1,0:T(1,128)} %reshape.52.place_ref.refs_0_, bf16[16,16,512]{2,1,0:T(8,128)(2,1)} %cot_hbm.1, bf16[16,16,512]{2,1,0:T(8,128)(2,1)} %residual_hbm.1, bf16[192,512]{1,0:T(8,128)(2,1)} %copy-done.14, ...), custom_call_target="tpu_custom_call" | custom-call | tf_op jit(solution)/shard_map/to_slots/pallas_call | solution.py:484
  22.4 7.7 %all-to-all-start.1 = ((bf16[32,16,512]{2,1,0:T(8,128)(2,1)}), bf16[32,16,512]{2,1,0:T(8,128)(2,1)S(1)}, u32[]{:S(2)}, u32[]{:S(2)}) async-start(bf16[32,16,512]{2,1,0:T(8,128)(2,1)} %bitcast.39), calls=%async_computation.1 | async-start | bytes 1048576 | tf_op jit(solution)/shard_map/all_to_all | solution.py:658
  30.1 8.0 %attend.1 = (bf16[64,512]{1,0:T(8,128)(2,1)}, bf16[64,512]{1,0:T(8,128)(2,1)}, bf16[64,512]{1,0:T(8,128)(2,1)}, bf16[64,512]{1,0:T(8,128)(2,1)}, bf16[16,256,256]{2,1,0:T(8,128)(2,1)}) custom-call(s32[1]{0:T(128)} %bitcast.2.last_ref, bf16[192,512]{1,0:T(8,128)(2,1)} %get-tuple-element.55.refs_0_, bf16[192,512]{1,0:T(8,128)(2,1)} %copy-done.14, ...), custom_call_target="tpu_custom_call" | custom-call | flops 536870912 | bytes 1572864 | tf_op jit(solution)/shard_map/attend/pallas_call | solution.py:166
  38.0 0.9 collective-permute-start.4
  38.9 1.0 collective-permute-start.5
  39.9 10.3 %collective-permute-done.3.refs_3_.refs_6_ = bf16[64,512]{1,0:T(8,128)(2,1)S(1)} collective-permute-done((bf16[64,512]{1,0:T(8,128)(2,1)}, bf16[64,512]{1,0:T(8,128)(2,1)S(1)}, u32[]{:S(2)}, u32[]{:S(2)}) %collective-permute-start.3) | collective-permute-done | bytes 65568 | tf_op jit(solution)/shard_map/ppermute | solution.py:37
  50.2 0.6 copy-done.11
  50.8 2.8 %norm.1 = (bf16[512,512]{1,0:T(8,128)(2,1)}, f32[256,512]{1,0:T(8,128)}, f32[256,1]{1,0:T(8,128)}) custom-call(s32[1,256]{1,0:T(1,128)} %reshape.52.place_ref.refs_0_, f32[1,512]{1,0:T(1,128)} %bitcast.42, bf16[512,512]{1,0:T(8,128)(2,1)} %refs_2_.5, bf16[64,512]{1,0:T(8,128)(2,1)} %copy-done.11, bf16[64,512]{1,0:T(8,128)(2,1)} %copy-done.12, ...), custom_call_target="tpu_custom_call" | custom-call | bytes 1 | tf_op jit(solution)/shard_map/norm/pallas_call | solution.py:147
  53.7 7.5 %all-to-all-start = ((bf16[32,16,512]{2,1,0:T(8,128)(2,1)}), bf16[32,16,512]{2,1,0:T(8,128)(2,1)S(1)}, u32[]{:S(2)}, u32[]{:S(2)}) async-start(bf16[32,16,512]{2,1,0:T(8,128)(2,1)} %bitcast.37), calls=%async_computation | async-start | bytes 1048576 | tf_op jit(solution)/shard_map/all_to_all | solution.py:658
  61.3 1.3 collective-permute-start.6
  62.6 0.7 convert_bitcast_fusion
  63.3 0.6 reshape.60.router_hbm.refs_4_
  63.9 0.6 pad_add_fusion.units_ref
  64.5 13.9 %all-to-all-done = bf16[32,16,512]{2,1,0:T(8,128)(2,1)S(1)} async-done(((bf16[32,16,512]{2,1,0:T(8,128)(2,1)}), bf16[32,16,512]{2,1,0:T(8,128)(2,1)S(1)}, u32[]{:S(2)}, u32[]{:S(2)}) %all-to-all-start) | async-done | bytes 524320 | tf_op jit(solution)/shard_map/all_to_all | solution.py:658
  78.5 1.5 collective-permute-start.7
  79.9 1.8 collective-permute-done.6.refs_0_.refs_3_
  81.7 0.8 copy-done.24
  82.5 11.3 %experts.1 = (bf16[2,256,512]{2,1,0:T(8,128)(2,1)}, f32[2,2,512]{2,1,0:T(2,128)}) custom-call(bf16[2,256,512]{2,1,0:T(8,128)(2,1)} %copy-done.10, bf16[2,256,512]{2,1,0:T(8,128)(2,1)} %copy-done.9, f32[2,1,512]{2,1,0:T(1,128)} %reshape.60.router_hbm.refs_4_, f32[1,512]{1,0:T(1,128)} %bitcast.43, bf16[2,512,2048]{2,1,0:T(8,128)(2,1)} %refs_5_.1, ...), custom_call_target="tpu_custom_call" | custom-call | flops 6442450944 | bytes 8388608 | tf_op jit(solution)/shard_map/experts/pallas_call | solution.py:256
  93.9 0.9 copy-done.8
  94.7 1.9 to_devices.1
  96.6 7.8 %all-to-all-start.2 = ((bf16[32,16,512]{2,1,0:T(8,128)(2,1)}), bf16[32,16,512]{2,1,0:T(8,128)(2,1)S(1)}, u32[]{:S(2)}, u32[]{:S(2)}) async-start(bf16[32,16,512]{2,1,0:T(8,128)(2,1)} %to_devices.1), calls=%async_computation.2 | async-start | bytes 1048576 | tf_op jit(solution)/shard_map/all_to_all | solution.py:681
  104.4 12.6 %weight_sums.1 = (bf16[2,512,256]{2,1,0:T(8,128)(2,1)}, bf16[2,512,256]{2,1,0:T(8,128)(2,1)}, bf16[2,2,512,256]{3,2,1,0:T(8,128)(2,1)}, bf16[2,2,512,256]{3,2,1,...) custom-call(s32[4]{0:T(128)} %pad_add_fusion.units_ref, bf16[2,256,512]{2,1,0:T(8,128)(2,1)} %copy-done.10, ...), custom_call_target="tpu_custom_call" | custom-call | flops 8589934592 | bytes 4194304 | tf_op jit(solution)/shard_map/weight_sums/pallas_call | solution.py:331
  117.2 3.2 %collective-permute-start.15 = (bf16[2,512,256]{2,1,0:T(8,128)(2,1)}, bf16[2,512,256]{2,1,0:T(8,128)(2,1)S(1)}, u32[]{:S(2)}, u32[]{:S(2)}) collective-permute-start(bf16[2,512,256]{2,1,0:T(8,128)(2,1)} %get-tuple-element.92), channel_id=1, source_target_pairs={{0,96},{32,0},{64,32},{96,64},{1,97},{33,1},{65,33},{97,65},{2,98}... | collective-permute-start | bytes 1572872 | tf_op jit(solution)/shard_map/ppermute | solution.py:46
  120.4 1.2 all-to-all-done.2
  121.6 0.8 copy-done.3
  122.4 3.3 %token_grads.1 = (bf16[64,512]{1,0:T(8,128)(2,1)}, bf16[64,512]{1,0:T(8,128)(2,1)}, bf16[64,512]{1,0:T(8,128)(2,1)}, bf16[64,512]{1,0:T(8,128)(2,1)}, bf16[64,51...) custom-call(s32[1,256]{1,0:T(1,128)} %reshape.52.place_ref.refs_0_, ...), custom_call_target="tpu_custom_call" | custom-call | bytes 1 | tf_op jit(solution)/shard_map/token_grads/pallas_call | solution.py:147
  125.7 7.1 %all-to-all-start.3 = ((bf16[32,16,512]{2,1,0:T(8,128)(2,1)}), bf16[32,16,512]{2,1,0:T(8,128)(2,1)S(1)}, u32[]{:S(2)}, u32[]{:S(2)}) async-start(bf16[32,16,512]{2,1,0:T(8,128)(2,1)} %bitcast.38), calls=%async_computation.3 | async-start | bytes 1048576 | tf_op jit(solution)/shard_map/all_to_all | solution.py:704
  132.9 2.5 %collective-permute-start.8 = (bf16[64,512]{1,0:T(8,128)(2,1)}, bf16[64,512]{1,0:T(8,128)(2,1)S(1)}, u32[]{:S(2)}, u32[]{:S(2)}) collective-permute-start(bf16[64,512]{1,0:T(8,128)(2,1)} %get-tuple-element.73), channel_id=1, source_target_pairs={{1,0},{2,1},{3,2},{4,3},{5,4},{6,5},{7,6},{8,7},{9,8},{10,9},{11,1... | collective-permute-start | bytes 196616 | tf_op jit(solution)/shard_map/ppermute | solution.py:29
  135.4 1.2 collective-permute-start.9
  136.7 7.9 %collective-permute-done.8.refs_5_.refs_4_ = bf16[64,512]{1,0:T(8,128)(2,1)S(1)} collective-permute-done((bf16[64,512]{1,0:T(8,128)(2,1)}, bf16[64,512]{1,0:T(8,128)(2,1)S(1)}, u32[]{:S(2)}, u32[]{:S(2)}) %collective-permute-start.8) | collective-permute-done | bytes 65568 | tf_op jit(solution)/shard_map/ppermute | solution.py:29
  144.6 1.7 collective-permute-done.10.refs_7_.refs_6_
  146.3 0.6 copy-done.22
  146.9 3.3 %join.1 = (bf16[2,2,512,256]{3,2,1,0:T(8,128)(2,1)}, bf16[2,2,512,256]{3,2,1,0:T(8,128)(2,1)}) custom-call(bf16[2,2,512,256]{3,2,1,0:T(8,128)(2,1)} %get-tuple-element.89.refs_0_, bf16[2,2,512,256]{3,2,1,0:T(8,128)(2,1)} %get-tuple-element.90.refs_1_, bf16[2,512,256]{2,1,0:T(8,128)(2,1)} %copy-done.6, bf16[2,512,256]{2,1,0:T(8,128)(2,1)} %copy-done.7, ...), custom_call_target="tpu_custom_call" | custom-call | bytes 1 | tf_op jit(solution)/shard_map/join/pallas_call | solution.py:147
  150.3 0.3 collective-permute-start.16
  150.6 3.2 %collective-permute-start.17 = (bf16[2,2,512,256]{3,2,1,0:T(8,128)(2,1)}, bf16[2,2,512,256]{3,2,1,0:T(8,128)(2,1)S(1)}, u32[]{:S(2)}, u32[]{:S(2)}) collective-permute-start(bf16[2,2,512,256]{3,2,1,0:T(8,128)(2,1)} %get-tuple-element.94), channel_id=1, source_target_pairs={{0,96},{32,0},{64,32},{96,64},{1,97},{33,1},{65,33},{97,65},{2,98}... | collective-permute-start | bytes 3145736 | tf_op jit(solution)/shard_map/ppermute | solution.py:46
  153.9 6.4 %attend_back.1 = (bf16[192,512]{1,0:T(8,128)(2,1)}, bf16[192,512]{1,0:T(8,128)(2,1)}, bf16[192,512]{1,0:T(8,128)(2,1)}, bf16[192,512]{1,0:T(8,128)(2,1)}) custom-call(bf16[192,512]{1,0:T(8,128)(2,1)} %get-tuple-element.55.refs_0_, bf16[192,512]{1,0:T(8,128)(2,1)} %copy-done.14, bf16[192,512]{1,0:T(8,128)(2,1)} %copy-done.15, bf16[192,512]{1,0:T(8,128)(2,1)} %copy-done.16, ...), custom_call_target="tpu_custom_call" | custom-call | flops 1073741824 | bytes 3145728 | tf_op jit(solution)/shard_map/attend_back/pallas_call | solution.py:186
  160.3 3.0 %collective-permute-start.12 = (bf16[192,512]{1,0:T(8,128)(2,1)}, bf16[192,512]{1,0:T(8,128)(2,1)S(1)}, u32[]{:S(2)}, u32[]{:S(2)}) collective-permute-start(bf16[192,512]{1,0:T(8,128)(2,1)} %get-tuple-element.78), channel_id=1, source_target_pairs={{224,0},{0,32},{32,64},{64,96},{96,128},{128,160},{160,192},{192,2... | collective-permute-start | bytes 589832 | tf_op jit(solution)/shard_map/ppermute | solution.py:31
  163.4 0.6 select_maximum_fusion.refs_1_
  164.0 0.8 copy-done.4
  164.8 1.8 share_sum.2
  166.6 7.1 %all-to-all-start.4 = ((bf16[8,24,512]{2,1,0:T(8,128)(2,1)}), bf16[8,24,512]{2,1,0:T(8,128)(2,1)S(1)}, u32[]{:S(2)}, u32[]{:S(2)}) async-start(bf16[8,24,512]{2,1,0:T(8,128)(2,1)} %share_sum.2), calls=%async_computation.4 | async-start | bytes 393216 | tf_op jit(solution)/shard_map/all_to_all | solution.py:705
  173.7 6.6 %collective-permute-done.11.refs_0_ = bf16[192,512]{1,0:T(8,128)(2,1)S(1)} collective-permute-done((bf16[192,512]{1,0:T(8,128)(2,1)}, bf16[192,512]{1,0:T(8,128)(2,1)S(1)}, u32[]{:S(2)}, u32[]{:S(2)}) %collective-permute-start.11) | collective-permute-done | bytes 196640 | tf_op jit(solution)/shard_map/ppermute | solution.py:37
  180.3 9.0 %collective-permute-done.12.refs_1_ = bf16[192,512]{1,0:T(8,128)(2,1)S(1)} collective-permute-done((bf16[192,512]{1,0:T(8,128)(2,1)}, bf16[192,512]{1,0:T(8,128)(2,1)S(1)}, u32[]{:S(2)}, u32[]{:S(2)}) %collective-permute-start.12) | collective-permute-done | bytes 196640 | tf_op jit(solution)/shard_map/ppermute | solution.py:31
  189.3 0.7 copy-done.18
  190.0 0.7 copy-done.19
  190.6 3.2 %tiles.2 = (bf16[16,16,512]{2,1,0:T(8,128)(2,1)}, bf16[16,16,512]{2,1,0:T(8,128)(2,1)}, bf16[16,16,512]{2,1,0:T(8,128)(2,1)}) custom-call(bf16[192,512]{1,0:T(8,128)(2,1)} %copy-done.17, bf16[192,512]{1,0:T(8,128)(2,1)} %copy-done.18, bf16[192,512]{1,0:T(8,128)(2,1)} %copy-done.19, bf16[192,512]{1,0:T(8,128)(2,1)} %get-tuple-element.80.refs_3_.refs_2_), custom_call_target="tpu_custom_call" | custom-call | tf_op jit(solution)/shard_map/tiles/pallas_call | solution.py:446
  193.9 1.0 copy-done
  195.2 1.9 share_sum.3
  197.1 8.3 %all-to-all-start.5 = ((bf16[32,24,512]{2,1,0:T(8,128)(2,1)}), bf16[32,24,512]{2,1,0:T(8,128)(2,1)S(1)}, u32[]{:S(2)}, u32[]{:S(2)}) async-start(bf16[32,24,512]{2,1,0:T(8,128)(2,1)} %share_sum.3), calls=%async_computation.5 | async-start | bytes 1572864 | tf_op jit(solution)/shard_map/all_to_all | solution.py:706
  205.4 2.8 %tiles.3 = bf16[16,16,512]{2,1,0:T(8,128)(2,1)} custom-call(bf16[64,512]{1,0:T(8,128)(2,1)} %get-tuple-element.84.refs_0_, bf16[64,512]{1,0:T(8,128)(2,1)} %get-tuple-element.85.refs_1_, bf16[64,512]{1,0:T(8,128)(2,1)} %get-tuple-element.86.refs_2_, bf16[64,512]{1,0:T(8,128)(2,1)} %get-tuple-element.87.refs_3_), custom_call_target="tpu_custom_call" | custom-call | tf_op jit(solution)/shard_map/tiles/pallas_call | solution.py:446
  208.3 3.1 %weight_total.1 = (bf16[2,512,256]{2,1,0:T(8,128)(2,1)}, bf16[2,256,512]{2,1,0:T(8,128)(2,1)}) custom-call(f32[2,2,512,256]{3,2,1,0:T(8,128)} %get-tuple-element.98.own_ref, bf16[2,2,512,256]{3,2,1,0:T(8,128)(2,1)} %copy-done, bf16[2,2,512,256]{3,2,1,0:T(8,128)(2,1)} %copy-done.1), custom_call_target="tpu_custom_call" | custom-call | tf_op jit(solution)/shard_map/weight_total/pallas_call | solution.py:381
  211.4 16.4 %all-to-all-done.5.refs_0_ = bf16[32,24,512]{2,1,0:T(8,128)(2,1)S(1)} async-done(((bf16[32,24,512]{2,1,0:T(8,128)(2,1)}), bf16[32,24,512]{2,1,0:T(8,128)(2,1)S(1)}, u32[]{:S(2)}, u32[]{:S(2)}) %all-to-all-start.5) | async-done | bytes 786464 | tf_op jit(solution)/shard_map/all_to_all | solution.py:706
  227.8 0.9 copy-done.2
  228.7 2.2 finish.1
  230.9 1.1 slice.11
  232.0 0.7 reshape.59
  (65 shorter events, 0.9 us)
Async XLA Ops:
  2.7 11.5 %collective-permute-start = (bf16[192,512]{1,0:T(8,128)(2,1)}, bf16[192,512]{1,0:T(8,128)(2,1)S(1)}, u32[]{:S(2)}, u32[]{:S(2)}) collective-permute-start(bf16[192,512]{1,0:T(8,128)(2,1)} %get-tuple-element.56), channel_id=1, source_target_pairs={{1,0},{2,1},{3,2},{4,3},{5,4},{6,5},{7,6},{8,7},{9,8},{10,9},{11,1... | collective-permute-start | bytes 589832 | tf_op jit(solution)/shard_map/ppermute | solution.py:29
  7.9 10.1 %collective-permute-start.1 = (bf16[192,512]{1,0:T(8,128)(2,1)}, bf16[192,512]{1,0:T(8,128)(2,1)S(1)}, u32[]{:S(2)}, u32[]{:S(2)}) collective-permute-start(bf16[192,512]{1,0:T(8,128)(2,1)} %get-tuple-element.57), channel_id=1, source_target_pairs={{32,0},{64,32},{96,64},{128,96},{160,128},{192,160},{224,192},{0,2... | collective-permute-start | bytes 589832 | tf_op jit(solution)/shard_map/ppermute | solution.py:31
  12.7 5.4 %collective-permute-start.2 = (bf16[192,512]{1,0:T(8,128)(2,1)}, bf16[192,512]{1,0:T(8,128)(2,1)S(1)}, u32[]{:S(2)}, u32[]{:S(2)}) collective-permute-start(bf16[192,512]{1,0:T(8,128)(2,1)} %get-tuple-element.58), channel_id=1, source_target_pairs={{33,0},{34,1},{35,2},{36,3},{37,4},{38,5},{39,6},{40,7},{41,8},{42... | collective-permute-start | bytes 589832 | tf_op jit(solution)/shard_map/ppermute | solution.py:37
  14.2 3.9 %copy-start.14 = (bf16[192,512]{1,0:T(8,128)(2,1)}, bf16[192,512]{1,0:T(8,128)(2,1)S(1)}, u32[]{:S(2)}) copy-start(bf16[192,512]{1,0:T(8,128)(2,1)S(1)} %collective-permute-done.refs_1_.refs_0_) | copy-start | bytes 589828
  18.1 0.7 copy-start.15
  18.7 0.7 copy-start.16
  22.4 31.3 %all-to-all-start.1 = ((bf16[32,16,512]{2,1,0:T(8,128)(2,1)}), bf16[32,16,512]{2,1,0:T(8,128)(2,1)S(1)}, u32[]{:S(2)}, u32[]{:S(2)}) async-start(bf16[32,16,512]{2,1,0:T(8,128)(2,1)} %bitcast.39), calls=%async_computation.1 | async-start | bytes 1048576 | tf_op jit(solution)/shard_map/all_to_all | solution.py:658
  38.0 12.1 %collective-permute-start.3 = (bf16[64,512]{1,0:T(8,128)(2,1)}, bf16[64,512]{1,0:T(8,128)(2,1)S(1)}, u32[]{:S(2)}, u32[]{:S(2)}) collective-permute-start(bf16[64,512]{1,0:T(8,128)(2,1)} %get-tuple-element.59), channel_id=1, source_target_pairs={{255,0},{224,1},{225,2},{226,3},{227,4},{228,5},{229,6},{230,7},{2... | collective-permute-start | bytes 196616 | tf_op jit(solution)/shard_map/ppermute | solution.py:37
  38.0 12.1 %collective-permute-start.4 = (bf16[64,512]{1,0:T(8,128)(2,1)}, bf16[64,512]{1,0:T(8,128)(2,1)S(1)}, u32[]{:S(2)}, u32[]{:S(2)}) collective-permute-start(bf16[64,512]{1,0:T(8,128)(2,1)} %get-tuple-element.60), channel_id=1, source_target_pairs={{224,0},{0,32},{32,64},{64,96},{96,128},{128,160},{160,192},{192,2... | collective-permute-start | bytes 196616 | tf_op jit(solution)/shard_map/ppermute | solution.py:31
  38.9 11.2 %collective-permute-start.5 = (bf16[64,512]{1,0:T(8,128)(2,1)}, bf16[64,512]{1,0:T(8,128)(2,1)S(1)}, u32[]{:S(2)}, u32[]{:S(2)}) collective-permute-start(bf16[64,512]{1,0:T(8,128)(2,1)} %get-tuple-element.61), channel_id=1, source_target_pairs={{31,0},{0,1},{1,2},{2,3},{3,4},{4,5},{5,6},{6,7},{7,8},{8,9},{9,10... | collective-permute-start | bytes 196616 | tf_op jit(solution)/shard_map/ppermute | solution.py:29
  50.2 0.6 copy-start.11
  50.2 0.6 copy-start.12
  50.2 0.7 copy-start.13
  53.7 24.7 %all-to-all-start = ((bf16[32,16,512]{2,1,0:T(8,128)(2,1)}), bf16[32,16,512]{2,1,0:T(8,128)(2,1)S(1)}, u32[]{:S(2)}, u32[]{:S(2)}) async-start(bf16[32,16,512]{2,1,0:T(8,128)(2,1)} %bitcast.37), calls=%async_computation | async-start | bytes 1048576 | tf_op jit(solution)/shard_map/all_to_all | solution.py:658
  61.3 20.4 %copy-start.9 = (bf16[2,256,512]{2,1,0:T(8,128)(2,1)}, bf16[2,256,512]{2,1,0:T(8,128)(2,1)S(1)}, u32[]{:S(2)}) copy-start(bf16[2,256,512]{2,1,0:T(8,128)(2,1)S(1)} %copy_bitcast_fusion.cot_hbm.refs_2_) | copy-start | bytes 1572868
  61.3 20.4 %collective-permute-start.6 = (bf16[2,256,512]{2,1,0:T(8,128)(2,1)S(1)}, bf16[2,256,512]{2,1,0:T(8,128)(2,1)S(1)}, u32[]{:S(2)}, u32[]{:S(2)}) collective-permute-start(bf16[2,256,512]{2,1,0:T(8,128)(2,1)S(1)} %copy_bitcast_fusion.cot_hbm.refs_2_), channel_id=1, source_target_pairs={{0,128},{128,0},{1,129},{129,1},{2,130},{130,2},{3,131},{131,3},{4... | collective-permute-start | bytes 1572872 | tf_op jit(solution)/shard_map/ppermute | solution.py:41
  78.4 3.3 %copy-start.10 = (bf16[2,256,512]{2,1,0:T(8,128)(2,1)}, bf16[2,256,512]{2,1,0:T(8,128)(2,1)S(1)}, u32[]{:S(2)}) copy-start(bf16[2,256,512]{2,1,0:T(8,128)(2,1)S(1)} %copy_bitcast_fusion.1.hidden_hbm.refs_0_) | copy-start | bytes 1572868
  78.5 15.4 %collective-permute-start.7 = (bf16[2,256,512]{2,1,0:T(8,128)(2,1)S(1)}, bf16[2,256,512]{2,1,0:T(8,128)(2,1)S(1)}, u32[]{:S(2)}, u32[]{:S(2)}) collective-permute-start(bf16[2,256,512]{2,1,0:T(8,128)(2,1)S(1)} %copy_bitcast_fusion.1.hidden_hbm.refs_0_), channel_id=1, source_target_pairs={{0,128},{128,0},{1,129},{129,1},{2,130},{130,2},{3,131},{131,3},{4... | collective-permute-start | bytes 1572872 | tf_op jit(solution)/shard_map/ppermute | solution.py:41
  81.7 0.8 copy-start.24
  93.9 0.9 copy-start.8
  96.6 25.0 %all-to-all-start.2 = ((bf16[32,16,512]{2,1,0:T(8,128)(2,1)}), bf16[32,16,512]{2,1,0:T(8,128)(2,1)S(1)}, u32[]{:S(2)}, u32[]{:S(2)}) async-start(bf16[32,16,512]{2,1,0:T(8,128)(2,1)} %to_devices.1), calls=%async_computation.2 | async-start | bytes 1048576 | tf_op jit(solution)/shard_map/all_to_all | solution.py:681
  117.1 36.8 %copy-start.23 = (f32[2,2,512]{2,1,0:T(2,128)S(1)}, f32[2,2,512]{2,1,0:T(2,128)}, u32[]{:S(2)}) copy-start(f32[2,2,512]{2,1,0:T(2,128)} %get-tuple-element.70.refs_7_) | copy-start | bytes 24580
  117.1 19.5 %collective-permute-start.14 = (bf16[2,512,256]{2,1,0:T(8,128)(2,1)}, bf16[2,512,256]{2,1,0:T(8,128)(2,1)S(1)}, u32[]{:S(2)}, u32[]{:S(2)}) collective-permute-start(bf16[2,512,256]{2,1,0:T(8,128)(2,1)} %get-tuple-element.91), channel_id=1, source_target_pairs={{0,32},{32,64},{64,96},{96,0},{1,33},{33,65},{65,97},{97,1},{2,34}... | collective-permute-start | bytes 1572872 | tf_op jit(solution)/shard_map/ppermute | solution.py:46
  117.2 19.4 %collective-permute-start.15 = (bf16[2,512,256]{2,1,0:T(8,128)(2,1)}, bf16[2,512,256]{2,1,0:T(8,128)(2,1)S(1)}, u32[]{:S(2)}, u32[]{:S(2)}) collective-permute-start(bf16[2,512,256]{2,1,0:T(8,128)(2,1)} %get-tuple-element.92), channel_id=1, source_target_pairs={{0,96},{32,0},{64,32},{96,64},{1,97},{33,1},{65,33},{97,65},{2,98}... | collective-permute-start | bytes 1572872 | tf_op jit(solution)/shard_map/ppermute | solution.py:46
  121.6 0.8 copy-start.3
  125.7 38.2 %all-to-all-start.3 = ((bf16[32,16,512]{2,1,0:T(8,128)(2,1)}), bf16[32,16,512]{2,1,0:T(8,128)(2,1)S(1)}, u32[]{:S(2)}, u32[]{:S(2)}) async-start(bf16[32,16,512]{2,1,0:T(8,128)(2,1)} %bitcast.38), calls=%async_computation.3 | async-start | bytes 1048576 | tf_op jit(solution)/shard_map/all_to_all | solution.py:704
  132.9 11.7 %collective-permute-start.8 = (bf16[64,512]{1,0:T(8,128)(2,1)}, bf16[64,512]{1,0:T(8,128)(2,1)S(1)}, u32[]{:S(2)}, u32[]{:S(2)}) collective-permute-start(bf16[64,512]{1,0:T(8,128)(2,1)} %get-tuple-element.73), channel_id=1, source_target_pairs={{1,0},{2,1},{3,2},{4,3},{5,4},{6,5},{7,6},{8,7},{9,8},{10,9},{11,1... | collective-permute-start | bytes 196616 | tf_op jit(solution)/shard_map/ppermute | solution.py:29
  135.4 9.2 %collective-permute-start.9 = (bf16[64,512]{1,0:T(8,128)(2,1)}, bf16[64,512]{1,0:T(8,128)(2,1)S(1)}, u32[]{:S(2)}, u32[]{:S(2)}) collective-permute-start(bf16[64,512]{1,0:T(8,128)(2,1)} %get-tuple-element.74), channel_id=1, source_target_pairs={{32,0},{64,32},{96,64},{128,96},{160,128},{192,160},{224,192},{0,2... | collective-permute-start | bytes 196616 | tf_op jit(solution)/shard_map/ppermute | solution.py:31
  136.6 9.7 %collective-permute-start.10 = (bf16[64,512]{1,0:T(8,128)(2,1)}, bf16[64,512]{1,0:T(8,128)(2,1)S(1)}, u32[]{:S(2)}, u32[]{:S(2)}) collective-permute-start(bf16[64,512]{1,0:T(8,128)(2,1)} %get-tuple-element.75), channel_id=1, source_target_pairs={{33,0},{34,1},{35,2},{36,3},{37,4},{38,5},{39,6},{40,7},{41,8},{42... | collective-permute-start | bytes 196616 | tf_op jit(solution)/shard_map/ppermute | solution.py:37
  136.6 9.7 %copy-start.6 = (bf16[2,512,256]{2,1,0:T(8,128)(2,1)}, bf16[2,512,256]{2,1,0:T(8,128)(2,1)S(1)}, u32[]{:S(2)}) copy-start(bf16[2,512,256]{2,1,0:T(8,128)(2,1)S(1)} %collective-permute-done.14.refs_2_) | copy-start | bytes 1572868
  136.6 9.6 %copy-start.7 = (bf16[2,512,256]{2,1,0:T(8,128)(2,1)}, bf16[2,512,256]{2,1,0:T(8,128)(2,1)S(1)}, u32[]{:S(2)}) copy-start(bf16[2,512,256]{2,1,0:T(8,128)(2,1)S(1)} %collective-permute-done.15.refs_3_) | copy-start | bytes 1572868
  144.6 1.7 copy-start.20
  144.6 1.7 copy-start.21
  146.3 0.6 copy-start.22
  150.3 43.6 %collective-permute-start.16 = (bf16[2,2,512,256]{3,2,1,0:T(8,128)(2,1)}, bf16[2,2,512,256]{3,2,1,0:T(8,128)(2,1)S(1)}, u32[]{:S(2)}, u32[]{:S(2)}) collective-permute-start(bf16[2,2,512,256]{3,2,1,0:T(8,128)(2,1)} %get-tuple-element.93.refs_3_), channel_id=1, source_target_pairs={{0,32},{32,64},{64,96},{96,0},{1,33},{33,65},{65,97},{97,1},{2,34}... | collective-permute-start | bytes 3145736 | tf_op jit(solution)/shard_map/ppermute | solution.py:46
  150.6 43.2 %collective-permute-start.17 = (bf16[2,2,512,256]{3,2,1,0:T(8,128)(2,1)}, bf16[2,2,512,256]{3,2,1,0:T(8,128)(2,1)S(1)}, u32[]{:S(2)}, u32[]{:S(2)}) collective-permute-start(bf16[2,2,512,256]{3,2,1,0:T(8,128)(2,1)} %get-tuple-element.94), channel_id=1, source_target_pairs={{0,96},{32,0},{64,32},{96,64},{1,97},{33,1},{65,33},{97,65},{2,98}... | collective-permute-start | bytes 3145736 | tf_op jit(solution)/shard_map/ppermute | solution.py:46
  160.3 20.1 %collective-permute-start.11 = (bf16[192,512]{1,0:T(8,128)(2,1)}, bf16[192,512]{1,0:T(8,128)(2,1)S(1)}, u32[]{:S(2)}, u32[]{:S(2)}) collective-permute-start(bf16[192,512]{1,0:T(8,128)(2,1)} %get-tuple-element.77), channel_id=1, source_target_pairs={{255,0},{224,1},{225,2},{226,3},{227,4},{228,5},{229,6},{230,7},{2... | collective-permute-start | bytes 589832 | tf_op jit(solution)/shard_map/ppermute | solution.py:37
  160.3 28.9 %collective-permute-start.12 = (bf16[192,512]{1,0:T(8,128)(2,1)}, bf16[192,512]{1,0:T(8,128)(2,1)S(1)}, u32[]{:S(2)}, u32[]{:S(2)}) collective-permute-start(bf16[192,512]{1,0:T(8,128)(2,1)} %get-tuple-element.78), channel_id=1, source_target_pairs={{224,0},{0,32},{32,64},{64,96},{96,128},{128,160},{160,192},{192,2... | collective-permute-start | bytes 589832 | tf_op jit(solution)/shard_map/ppermute | solution.py:31
  163.4 25.9 %collective-permute-start.13 = (bf16[192,512]{1,0:T(8,128)(2,1)}, bf16[192,512]{1,0:T(8,128)(2,1)S(1)}, u32[]{:S(2)}, u32[]{:S(2)}) collective-permute-start(bf16[192,512]{1,0:T(8,128)(2,1)} %get-tuple-element.79), channel_id=1, source_target_pairs={{31,0},{0,1},{1,2},{2,3},{3,4},{4,5},{5,6},{6,7},{7,8},{8,9},{9,10... | collective-permute-start | bytes 589832 | tf_op jit(solution)/shard_map/ppermute | solution.py:29
  164.0 0.8 copy-start.4
  166.6 27.2 %all-to-all-start.4 = ((bf16[8,24,512]{2,1,0:T(8,128)(2,1)}), bf16[8,24,512]{2,1,0:T(8,128)(2,1)S(1)}, u32[]{:S(2)}, u32[]{:S(2)}) async-start(bf16[8,24,512]{2,1,0:T(8,128)(2,1)} %share_sum.2), calls=%async_computation.4 | async-start | bytes 393216 | tf_op jit(solution)/shard_map/all_to_all | solution.py:705
  180.3 9.0 %copy-start.17 = (bf16[192,512]{1,0:T(8,128)(2,1)}, bf16[192,512]{1,0:T(8,128)(2,1)S(1)}, u32[]{:S(2)}) copy-start(bf16[192,512]{1,0:T(8,128)(2,1)S(1)} %collective-permute-done.11.refs_0_) | copy-start | bytes 589828
  189.3 0.7 copy-start.18
  190.0 0.7 copy-start.19
  193.8 1.0 copy-start
  193.8 1.3 copy-start.1
  193.9 1.3 copy-start.5
  197.1 30.7 %all-to-all-start.5 = ((bf16[32,24,512]{2,1,0:T(8,128)(2,1)}), bf16[32,24,512]{2,1,0:T(8,128)(2,1)S(1)}, u32[]{:S(2)}, u32[]{:S(2)}) async-start(bf16[32,24,512]{2,1,0:T(8,128)(2,1)} %share_sum.3), calls=%async_computation.5 | async-start | bytes 1572864 | tf_op jit(solution)/shard_map/all_to_all | solution.py:706
  227.8 0.9 copy-start.2
